TPU v7x, 32 devices: a whole 2x2x4 slice. The times are simulated.
32 devices in a mesh: dp: 4 (over z), row: 4 (over x, core), col: 2 (over y).
Axes of the slice: x: 2, y: 2, z: 4, core: 2. Of those that a mesh axis runs over, the one named last changes fastest.
Arguments:
- latents_in: bfloat16 [8192, 1152], P(('dp', 'row'), 'col'), may hold values from -6 to 6
- text_emb: bfloat16 [960, 1152], P('dp', 'col'), may hold values from -6 to 6
- time_emb: bfloat16 [8, 6, 1152], P('dp', None, 'col'), may hold values from -3 to 3
- shift_table: bfloat16 [6, 1152], P(None, 'col'), may hold values from -3 to 3
- q_weight: bfloat16 [1152, 1152], P('col', 'row'), may hold values from -0.1875 to 0.1875
- k_weight: bfloat16 [1152, 1152], P('col', 'row'), may hold values from -0.1875 to 0.1875
- v_weight: bfloat16 [1152, 1152], P('col', 'row'), may hold values from -0.1875 to 0.1875
- q_bias: bfloat16 [1152], P(('row', 'col')), may hold values from -3 to 3
- v_bias: bfloat16 [1152], P(('row', 'col')), may hold values from -3 to 3
- o_weight: bfloat16 [1152, 1152], P('row', 'col'), may hold values from -0.5 to 0.5
- o_bias: bfloat16 [1152], P('col'), may hold values from -2 to 2
- cq_weight: bfloat16 [1152, 1152], P('col', 'row'), may hold values from -0.1875 to 0.1875
- cq_bias: bfloat16 [1152], P(('row', 'col')), may hold values from -3 to 3
- ck_weight: bfloat16 [1152, 1152], P('col', 'row'), may hold values from -0.1875 to 0.1875
- cv_weight: bfloat16 [1152, 1152], P('col', 'row'), may hold values from -0.1875 to 0.1875
- cv_bias: bfloat16 [1152], P(('row', 'col')), may hold values from -3 to 3
- co_weight: bfloat16 [1152, 1152], P('row', 'col'), may hold values from -0.5 to 0.5
- co_bias: bfloat16 [1152], P('col'), may hold values from -2 to 2
- up_weight: bfloat16 [1152, 4608], P('col', 'row'), may hold values from -0.1875 to 0.1875
- up_bias: bfloat16 [4608], P(('row', 'col')), may hold values from -3 to 3
- down_weight: bfloat16 [4608, 1152], P('row', 'col'), may hold values from -0.09375 to 0.09375
- down_bias: bfloat16 [1152], P('col'), may hold values from -4 to 4
- cotangent: bfloat16 [8192, 1152], P(('dp', 'row'), 'col'), may hold values from -6 to 6
Outputs:
- layer_out: bfloat16 [8192, 1152], P(('dp', 'row'), 'col')
- token_input_gradient: float32 [8192, 1152], P(('dp', 'row'), 'col')
- text_grad: float32 [960, 1152], P('dp', 'col')
- time_grad: float32 [8, 6, 1152], P('dp', None, 'col')
- table_grad: float32 [6, 1152], P(None, 'col')
- q_weight_grad: float32 [1152, 1152], P('col', 'row')
- k_weight_grad: float32 [1152, 1152], P('col', 'row')
- v_weight_grad: float32 [1152, 1152], P('col', 'row')
- q_bias_grad: float32 [1152], P(('row', 'col'))
- v_bias_grad: float32 [1152], P(('row', 'col'))
- o_weight_grad: float32 [1152, 1152], P('row', 'col')
- o_bias_grad: float32 [1152], P('col')
- cq_weight_grad: float32 [1152, 1152], P('col', 'row')
- cq_bias_grad: float32 [1152], P(('row', 'col'))
- ck_weight_grad: float32 [1152, 1152], P('col', 'row')
- cv_weight_grad: float32 [1152, 1152], P('col', 'row')
- cv_bias_grad: float32 [1152], P(('row', 'col'))
- co_weight_grad: float32 [1152, 1152], P('row', 'col')
- co_bias_grad: float32 [1152], P('col')
- up_weight_grad: float32 [1152, 4608], P('col', 'row')
- up_bias_grad: float32 [4608], P(('row', 'col'))
- down_weight_grad: float32 [4608, 1152], P('row', 'col')
- down_bias_grad: float32 [1152], P('col')
All inputs are finite; a program needn't handle non-finite values.
Results may differ from a plain program's by a relative error of at most 0.025.
Values may be sent and summed in bfloat16 or wider, within the bound.
No kernel may reach another device: no remote copies, remote signals or barrier semaphores. Data moves between devices by JAX's collectives and lax.ppermute only.
A program may use at most 192 MiB of HBM per device.

v0:
```python
import jax
import jax.numpy as jnp
from jax import lax
from jax.sharding import PartitionSpec as P

D = 1152
HD = 72
SEQ = 1024
TXT = 120
LAT_DEV = 2


HIGHEST = lax.Precision.HIGHEST
FLOAT = jnp.float32
BRAIN_FLOAT_TYPE = jnp.bfloat16
EPSILON = 1e-06


def plain_dot(left, right):
    return jnp.dot(left, right, preferred_element_type=FLOAT)


def lead_dot(left, right):
    return lax.dot_general(left, right, (((0,), (0,)), ((), ())), preferred_element_type=FLOAT)


def tail_dot(left, right):
    return lax.dot_general(left, right, (((1,), (1,)), ((), ())), preferred_element_type=FLOAT)


def rows_in(value):
    return lax.all_gather(value, "row", axis=0, tiled=True)


def rows_out(terms, tok_rows):
    return lax.psum_scatter(
        terms(jnp.int32(0), tok_rows * lax.axis_size("row")), "row", scatter_dimension=0, tiled=True
    )


def heads_in(value):
    return lax.all_gather(value, "col", axis=1, tiled=True)


def head_sums(value):
    return lax.psum_scatter(value, "col", scatter_dimension=1, tiled=True)


def hidden_sums(value):
    return lax.psum_scatter(
        value.astype(jnp.bfloat16), "col", scatter_dimension=1, tiled=True
    ).astype(jnp.float32)


def hidden_in(value):
    return lax.all_gather(value, "col", axis=1, tiled=True)


def col_sums(first, second):
    return lax.psum((first, second), "col")


def norm_forward(values):
    summed, squares = col_sums(
        jnp.sum(values, 1, keepdims=True), jnp.sum(values * values, 1, keepdims=True)
    )
    average = summed / D
    inv_std = lax.rsqrt(squares / D - average * average + EPSILON)
    return ((values - average) * inv_std, inv_std)


def layernorm_reverse(grad_norm, normed, inv_std):
    summed, crossed = col_sums(
        jnp.sum(grad_norm, 1, keepdims=True), jnp.sum(grad_norm * normed, 1, keepdims=True)
    )
    return inv_std * (grad_norm - summed / D - normed * crossed / D)


def gelu_tanh(values):
    return jax.nn.gelu(values, approximate=True)


def split_latents(value, length):
    return value.reshape(LAT_DEV, length, value.shape[1] // HD, HD)


def attend_forward(query, keys, values, length):

    def single(pieces):
        q_lat, k_lat, v_lat = pieces
        scores = jnp.einsum("qhd,khd->hqk", q_lat, k_lat, preferred_element_type=FLOAT) * HD ** (
            -0.5
        )
        peak_score = jnp.max(scores, 2, keepdims=True)
        raised = jnp.exp(scores - peak_score)
        summed = jnp.sum(raised, 2, keepdims=True)
        weights = (raised / summed).astype(BRAIN_FLOAT_TYPE)
        mixed = jnp.einsum("hqk,khd->qhd", weights, v_lat, preferred_element_type=FLOAT)
        return (mixed.astype(BRAIN_FLOAT_TYPE), (peak_score + jnp.log(summed))[:, :, 0])

    mixed, logsum = lax.map(
        single,
        (split_latents(query, SEQ), split_latents(keys, length), split_latents(values, length)),
    )
    return (mixed.reshape(query.shape), logsum)


def attend_backward(query, keys, values, logsum, grad_out, length):

    def single(pieces):
        q_lat, k_lat, v_lat, l_lat, g_lat = pieces
        scores = jnp.einsum("qhd,khd->hqk", q_lat, k_lat, preferred_element_type=FLOAT) * HD ** (
            -0.5
        )
        prob_full = jnp.exp(scores - l_lat[:, :, None])
        grad_prob = jnp.einsum("qhd,khd->hqk", g_lat, v_lat, preferred_element_type=FLOAT)
        centre = jnp.sum(prob_full * grad_prob, 2, keepdims=True)
        grad_score = (prob_full * (grad_prob - centre)).astype(BRAIN_FLOAT_TYPE)
        grad_query = jnp.einsum(
            "hqk,khd->qhd", grad_score, k_lat, preferred_element_type=FLOAT
        ) * HD ** (-0.5)
        grad_key = jnp.einsum(
            "hqk,qhd->khd", grad_score, q_lat, preferred_element_type=FLOAT
        ) * HD ** (-0.5)
        grad_value = jnp.einsum(
            "hqk,qhd->khd", prob_full.astype(BRAIN_FLOAT_TYPE), g_lat, preferred_element_type=FLOAT
        )
        return (
            grad_query.astype(BRAIN_FLOAT_TYPE),
            grad_key.astype(BRAIN_FLOAT_TYPE),
            grad_value.astype(BRAIN_FLOAT_TYPE),
        )

    results = lax.map(
        single,
        (
            split_latents(query, SEQ),
            split_latents(keys, length),
            split_latents(values, length),
            logsum,
            split_latents(grad_out, SEQ),
        ),
    )
    return (
        results[0].reshape(query.shape),
        results[1].reshape(keys.shape),
        results[2].reshape(values.shape),
    )


def on_device(
    latents_in,
    text_emb,
    time_emb,
    shift_table,
    q_weight,
    k_weight,
    v_weight,
    q_bias,
    v_bias,
    o_weight,
    o_bias,
    cq_weight,
    cq_bias,
    ck_weight,
    cv_weight,
    cv_bias,
    co_weight,
    co_bias,
    up_weight,
    up_bias,
    down_weight,
    down_bias,
    cotangent,
):
    tok_rows, width_col = latents_in.shape
    positions = lax.axis_index("row") * tok_rows + jnp.arange(tok_rows)
    member = (positions[:, None] // SEQ == jnp.arange(LAT_DEV)[None, :]).astype(FLOAT)
    modulation = shift_table.astype(FLOAT)[None] + time_emb.astype(FLOAT)
    token_wise = jnp.dot(
        member, modulation.reshape(LAT_DEV, 6 * width_col), precision=HIGHEST
    ).reshape(tok_rows, 6, width_col)
    selfattn_offset = token_wise[:, 0]
    selfattn_scale = token_wise[:, 1]
    selfattn_gate = token_wise[:, 2]
    shift_mlp = token_wise[:, 3]
    scale_mlp = token_wise[:, 4]
    gate_mlp = token_wise[:, 5]
    residual_value = latents_in.astype(FLOAT)
    first_normed, first_inverse_deviation = norm_forward(residual_value)
    first_hidden = (first_normed * (1.0 + selfattn_scale) + selfattn_offset).astype(
        BRAIN_FLOAT_TYPE
    )
    h_one_all = rows_in(first_hidden)
    projected = (
        lax.psum_scatter(plain_dot(h_one_all, q_weight), "col", scatter_dimension=1, tiled=True),
        lax.psum_scatter(plain_dot(h_one_all, k_weight), "col", scatter_dimension=1, tiled=True),
        lax.psum_scatter(plain_dot(h_one_all, v_weight), "col", scatter_dimension=1, tiled=True),
        lax.psum_scatter(plain_dot(text_emb, ck_weight), "col", scatter_dimension=1, tiled=True),
        lax.psum_scatter(plain_dot(text_emb, cv_weight), "col", scatter_dimension=1, tiled=True),
    )
    query = (projected[0] + q_bias.astype(FLOAT)).astype(BRAIN_FLOAT_TYPE)
    keys = projected[1].astype(BRAIN_FLOAT_TYPE)
    values = (projected[2] + v_bias.astype(FLOAT)).astype(BRAIN_FLOAT_TYPE)
    text_keys = projected[3].astype(BRAIN_FLOAT_TYPE)
    text_values = (projected[4] + cv_bias.astype(FLOAT)).astype(BRAIN_FLOAT_TYPE)
    attended, self_lse = attend_forward(query, keys, values, SEQ)
    attended_all = heads_in(attended)

    def self_term(start, count):
        return plain_dot(attended_all, o_weight)

    attention_result = rows_out(self_term, tok_rows) + o_bias.astype(FLOAT)
    first_residual = residual_value + selfattn_gate * attention_result
    cross_all = rows_in(first_residual.astype(BRAIN_FLOAT_TYPE))
    cross_query = (head_sums(plain_dot(cross_all, cq_weight)) + cq_bias.astype(FLOAT)).astype(
        BRAIN_FLOAT_TYPE
    )
    cross_att, cross_lse = attend_forward(cross_query, text_keys, text_values, TXT)
    cross_att_all = heads_in(cross_att)

    def cross_term(start, count):
        return plain_dot(cross_att_all, co_weight)

    x_two = first_residual + rows_out(cross_term, tok_rows) + co_bias.astype(FLOAT)
    norm_two, inv_two = norm_forward(x_two)
    h_two = (norm_two * (1.0 + scale_mlp) + shift_mlp).astype(BRAIN_FLOAT_TYPE)
    h_two_all = rows_in(h_two)
    pre_act = hidden_sums(plain_dot(h_two_all, up_weight)) + up_bias.astype(FLOAT)
    activated, gelu_pull = jax.vjp(gelu_tanh, pre_act)
    hidden_own = activated.astype(BRAIN_FLOAT_TYPE)
    hidden_all = hidden_in(hidden_own)

    def down_term(start, count):
        return plain_dot(hidden_all, down_weight)

    mlp_out = rows_out(down_term, tok_rows) + down_bias.astype(FLOAT)
    layer_out = (x_two + gate_mlp * mlp_out).astype(BRAIN_FLOAT_TYPE)
    grad_three = cotangent.astype(FLOAT)
    grad_mlp = (gate_mlp * grad_three).astype(BRAIN_FLOAT_TYPE)
    grad_gate_mlp = grad_three * mlp_out
    grad_mlp_all = rows_in(grad_mlp)
    down_weight_grad = lead_dot(hidden_all, grad_mlp_all)
    down_bias_part = jnp.sum(grad_mlp, 0, dtype=FLOAT)
    grad_pre = gelu_pull(hidden_sums(tail_dot(grad_mlp_all, down_weight)))[0].astype(
        BRAIN_FLOAT_TYPE
    )
    up_bias_grad = jnp.sum(grad_pre, 0, dtype=FLOAT)
    grad_pre_all = hidden_in(grad_pre)
    up_weight_grad = lead_dot(h_two_all, grad_pre_all)

    def up_term(start, count):
        return tail_dot(grad_pre_all, up_weight)

    grad_h_two = rows_out(up_term, tok_rows)
    grad_x_two = grad_three + layernorm_reverse(grad_h_two * (1.0 + scale_mlp), norm_two, inv_two)
    grad_cross = grad_x_two.astype(BRAIN_FLOAT_TYPE)
    grad_cross_all = rows_in(grad_cross)
    co_weight_grad = lead_dot(cross_att_all, grad_cross_all)
    co_bias_part = jnp.sum(grad_cross, 0, dtype=FLOAT)
    grad_cross_att = head_sums(tail_dot(grad_cross_all, co_weight)).astype(BRAIN_FLOAT_TYPE)
    grad_cross_query, grad_text_keys, grad_text_values = attend_backward(
        cross_query, text_keys, text_values, cross_lse, grad_cross_att, TXT
    )
    grad_cq_all = heads_in(grad_cross_query)
    cq_weight_grad = lead_dot(cross_all, grad_cq_all)
    cq_bias_grad = jnp.sum(grad_cross_query, 0, dtype=FLOAT)

    def cq_term(start, count):
        return tail_dot(grad_cq_all, cq_weight)

    first_residual_gradient = grad_x_two + rows_out(cq_term, tok_rows)
    attention_result_gradient = (selfattn_gate * first_residual_gradient).astype(BRAIN_FLOAT_TYPE)
    selfattn_gate_gradient = first_residual_gradient * attention_result
    grad_attn_all = rows_in(attention_result_gradient)
    o_weight_grad = lead_dot(attended_all, grad_attn_all)
    o_bias_part = jnp.sum(attention_result_gradient, 0, dtype=FLOAT)
    grad_att = head_sums(tail_dot(grad_attn_all, o_weight)).astype(BRAIN_FLOAT_TYPE)
    grad_query, grad_keys, grad_values = attend_backward(
        query, keys, values, self_lse, grad_att, SEQ
    )
    gq_all, gk_all, gv_all, gtk_all, gtv_all = (
        lax.all_gather(grad_query, "col", axis=1, tiled=True),
        lax.all_gather(grad_keys, "col", axis=1, tiled=True),
        lax.all_gather(grad_values, "col", axis=1, tiled=True),
        lax.all_gather(grad_text_keys, "col", axis=1, tiled=True),
        lax.all_gather(grad_text_values, "col", axis=1, tiled=True),
    )
    q_weight_grad = lead_dot(h_one_all, gq_all)
    k_weight_grad = lead_dot(h_one_all, gk_all)
    v_weight_grad = lead_dot(h_one_all, gv_all)
    q_bias_grad = jnp.sum(grad_query, 0, dtype=FLOAT)
    v_bias_grad = jnp.sum(grad_values, 0, dtype=FLOAT)
    ck_weight_grad = lead_dot(text_emb, gtk_all)
    cv_weight_grad = lead_dot(text_emb, gtv_all)
    cv_bias_grad = jnp.sum(grad_text_values, 0, dtype=FLOAT)
    text_part = tail_dot(gtk_all, ck_weight) + tail_dot(gtv_all, cv_weight)

    def qkv_term(start, count):
        return tail_dot(gq_all, q_weight) + tail_dot(gk_all, k_weight) + tail_dot(gv_all, v_weight)

    first_hidden_gradient = rows_out(qkv_term, tok_rows)
    token_input_gradient = first_residual_gradient + layernorm_reverse(
        first_hidden_gradient * (1.0 + selfattn_scale), first_normed, first_inverse_deviation
    )
    stacked = jnp.stack(
        (
            first_hidden_gradient,
            first_hidden_gradient * first_normed,
            selfattn_gate_gradient,
            grad_h_two,
            grad_h_two * norm_two,
            grad_gate_mlp,
        ),
        1,
    ).reshape(tok_rows, 6 * width_col)
    time_part = lax.dot_general(
        member, stacked, (((0,), (0,)), ((), ())), precision=HIGHEST, preferred_element_type=FLOAT
    )
    text_grad, time_grad, o_bias_grad, co_bias_grad, down_bias_grad = (
        lax.psum(text_part.astype(jnp.bfloat16), "row").astype(jnp.float32),
        lax.psum(time_part.astype(jnp.bfloat16), "row").astype(jnp.float32),
        lax.psum(o_bias_part.astype(jnp.bfloat16), "row").astype(jnp.float32),
        lax.psum(co_bias_part.astype(jnp.bfloat16), "row").astype(jnp.float32),
        lax.psum(down_bias_part.astype(jnp.bfloat16), "row").astype(jnp.float32),
    )
    time_grad = time_grad.reshape(LAT_DEV, 6, width_col)
    table_part = jnp.sum(time_grad, 0)
    summed_grads = (
        lax.psum(table_part.astype(jnp.bfloat16), "dp").astype(jnp.float32),
        lax.psum(q_weight_grad.astype(jnp.bfloat16), "dp").astype(jnp.float32),
        lax.psum(k_weight_grad.astype(jnp.bfloat16), "dp").astype(jnp.float32),
        lax.psum(v_weight_grad.astype(jnp.bfloat16), "dp").astype(jnp.float32),
        lax.psum(q_bias_grad.astype(jnp.bfloat16), "dp").astype(jnp.float32),
        lax.psum(v_bias_grad.astype(jnp.bfloat16), "dp").astype(jnp.float32),
        lax.psum(o_weight_grad.astype(jnp.bfloat16), "dp").astype(jnp.float32),
        lax.psum(o_bias_grad.astype(jnp.bfloat16), "dp").astype(jnp.float32),
        lax.psum(cq_weight_grad.astype(jnp.bfloat16), "dp").astype(jnp.float32),
        lax.psum(cq_bias_grad.astype(jnp.bfloat16), "dp").astype(jnp.float32),
        lax.psum(ck_weight_grad.astype(jnp.bfloat16), "dp").astype(jnp.float32),
        lax.psum(cv_weight_grad.astype(jnp.bfloat16), "dp").astype(jnp.float32),
        lax.psum(cv_bias_grad.astype(jnp.bfloat16), "dp").astype(jnp.float32),
        lax.psum(co_weight_grad.astype(jnp.bfloat16), "dp").astype(jnp.float32),
        lax.psum(co_bias_grad.astype(jnp.bfloat16), "dp").astype(jnp.float32),
        lax.psum(up_weight_grad.astype(jnp.bfloat16), "dp").astype(jnp.float32),
        lax.psum(up_bias_grad.astype(jnp.bfloat16), "dp").astype(jnp.float32),
        lax.psum(down_weight_grad.astype(jnp.bfloat16), "dp").astype(jnp.float32),
        lax.psum(down_bias_grad.astype(jnp.bfloat16), "dp").astype(jnp.float32),
    )
    return (layer_out, token_input_gradient, text_grad, time_grad) + tuple(summed_grads)


def solution(mesh):
    in_specs = (
        P(("dp", "row"), "col"),
        P("dp", "col"),
        P("dp", None, "col"),
        P(None, "col"),
        P("col", "row"),
        P("col", "row"),
        P("col", "row"),
        P(("row", "col")),
        P(("row", "col")),
        P("row", "col"),
        P("col"),
        P("col", "row"),
        P(("row", "col")),
        P("col", "row"),
        P("col", "row"),
        P(("row", "col")),
        P("row", "col"),
        P("col"),
        P("col", "row"),
        P(("row", "col")),
        P("row", "col"),
        P("col"),
        P(("dp", "row"), "col"),
    )
    out_specs = (
        P(("dp", "row"), "col"),
        P(("dp", "row"), "col"),
        P("dp", "col"),
        P("dp", None, "col"),
        P(None, "col"),
        P("col", "row"),
        P("col", "row"),
        P("col", "row"),
        P(("row", "col")),
        P(("row", "col")),
        P("row", "col"),
        P("col"),
        P("col", "row"),
        P(("row", "col")),
        P("col", "row"),
        P("col", "row"),
        P(("row", "col")),
        P("row", "col"),
        P("col"),
        P("col", "row"),
        P(("row", "col")),
        P("row", "col"),
        P("col"),
    )
    return jax.shard_map(
        on_device, mesh=mesh, in_specs=in_specs, out_specs=out_specs, check_vma=False
    )
```

profile of v0, /device:TPU:0, one launch (start us, length us, event | category | flops | bytes accessed | tf_op | source)
XLA Modules:
  0.0 1552.1 jit_solution(12672176876380601991)
XLA Ops:
  10.3 5.8 all-reduce.3
  23.2 25.9 %all-gather.15.cloned.1.call-done = bf16[2048,576]{0,1:T(8,128)(2,1)} async-done(((bf16[512,576]{0,1:T(8,128)(2,1)}), bf16[2048,576]{0,1:T(8,128)(2,1)}) %all-gather.15.cloned.1.call-update) | async-done | bytes 2359312 | tf_op jit(solution)/shard_map/all_gather | solution.py:32
  49.2 4.2 fusion.166
  54.3 4.2 fusion.167
  59.5 4.5 fusion.168
  64.7 23.6 %reduce-scatter.17.cloned.1.call-done = f32[2048,144]{0,1:T(8,128)} async-done(((f32[2048,288]{0,1:T(8,128)}), f32[2048,144]{0,1:T(8,128)}) %reduce-scatter.17.cloned.1.call-update) | async-done | bytes 1179664 | tf_op jit(solution)/shard_map/reduce_scatter | solution.py:198
  91.0 34.9 %reduce-scatter.19.cloned.1.call-done = f32[2048,144]{0,1:T(8,128)} async-done(((f32[2048,288]{0,1:T(8,128)}), f32[2048,144]{0,1:T(8,128)}) %reduce-scatter.19.cloned.1.call-update) | async-done | bytes 1179664 | tf_op jit(solution)/shard_map/reduce_scatter | solution.py:196
  127.9 34.9 %reduce-scatter.21.cloned.1.call-done = f32[2048,144]{0,1:T(8,128)} async-done(((f32[2048,288]{0,1:T(8,128)}), f32[2048,144]{0,1:T(8,128)}) %reduce-scatter.21.cloned.1.call-update) | async-done | bytes 1179664 | tf_op jit(solution)/shard_map/reduce_scatter | solution.py:197
  168.0 10.7 while.52
  181.5 22.9 %all-gather.17.cloned.1.call-done = bf16[2048,288]{0,1:T(8,128)(2,1)} async-done(((bf16[2048,144]{0,1:T(8,128)(2,1)}), bf16[2048,288]{0,1:T(8,128)(2,1)}) %all-gather.17.cloned.1.call-update) | async-done | bytes 1179664 | tf_op jit(solution)/shard_map/all_gather | solution.py:42
  204.3 4.8 fusion.160
  209.9 47.3 %reduce-scatter.23.cloned.1.call-done = f32[512,576]{0,1:T(8,128)} async-done(((f32[2048,576]{0,1:T(8,128)}), f32[512,576]{0,1:T(8,128)}) %reduce-scatter.23.cloned.1.call-update) | async-done | bytes 1179664 | tf_op jit(solution)/shard_map/reduce_scatter | solution.py:36
  264.1 20.0 %all-gather.19.cloned.1.call-done = bf16[2048,576]{0,1:T(8,128)(2,1)} async-done(((bf16[512,576]{0,1:T(8,128)(2,1)}), bf16[2048,576]{0,1:T(8,128)(2,1)}) %all-gather.19.cloned.1.call-update) | async-done | bytes 2359312 | tf_op jit(solution)/shard_map/all_gather | solution.py:32
  284.1 4.2 fusion.170
  289.0 10.0 reduce-scatter.29.cloned.1.call-done
  300.1 13.9 reduce-scatter.25.cloned.1.call-done
  315.7 35.6 %reduce-scatter.27.cloned.1.call-done = f32[2048,144]{0,1:T(8,128)} async-done(((f32[2048,288]{0,1:T(8,128)}), f32[2048,144]{0,1:T(8,128)}) %reduce-scatter.27.cloned.1.call-update) | async-done | bytes 1179664 | tf_op jit(solution)/shard_map/reduce_scatter | solution.py:46
  356.1 4.7 while.53
  363.6 22.9 %all-gather.21.cloned.1.call-done = bf16[2048,288]{0,1:T(8,128)(2,1)} async-done(((bf16[2048,144]{0,1:T(8,128)(2,1)}), bf16[2048,288]{0,1:T(8,128)(2,1)}) %all-gather.21.cloned.1.call-update) | async-done | bytes 1179664 | tf_op jit(solution)/shard_map/all_gather | solution.py:42
  386.5 4.8 fusion.161
  392.7 46.6 %reduce-scatter.31.cloned.1.call-done = f32[512,576]{0,1:T(8,128)} async-done(((f32[2048,576]{0,1:T(8,128)}), f32[512,576]{0,1:T(8,128)}) %reduce-scatter.31.cloned.1.call-update) | async-done | bytes 1179664 | tf_op jit(solution)/shard_map/reduce_scatter | solution.py:36
  439.3 4.2 fusion.149
  443.5 5.6 all-reduce.2
  456.8 21.1 %all-gather.23.cloned.1.call-done = bf16[2048,576]{0,1:T(8,128)(2,1)} async-done(((bf16[512,576]{0,1:T(8,128)(2,1)}), bf16[2048,576]{0,1:T(8,128)(2,1)}) %all-gather.23.cloned.1.call-update) | async-done | bytes 2359312 | tf_op jit(solution)/shard_map/all_gather | solution.py:32
  477.9 8.0 convolution_convert_fusion.3
  486.0 18.0 %all-gather.27.cloned.1.call-done = bf16[2048,576]{0,1:T(8,128)(2,1)} async-done(((bf16[512,576]{0,1:T(8,128)(2,1)}), bf16[2048,576]{0,1:T(8,128)(2,1)}) %all-gather.27.cloned.1.call-update) | async-done | bytes 2359312 | tf_op jit(solution)/shard_map/all_gather | solution.py:32
  504.0 7.1 convolution_convert_fusion.2
  512.5 53.7 %reduce-scatter.33.cloned.1.call-done = bf16[2048,576]{0,1:T(8,128)(2,1)} async-done(((bf16[2048,1152]{0,1:T(8,128)(2,1)}), bf16[2048,576]{0,1:T(8,128)(2,1)}) %reduce-scatter.33.cloned.1.call-update) | async-done | bytes 2359312 | tf_op jit(solution)/shard_map/reduce_scatter | solution.py:50
  566.2 4.2 multiply_convert_fusion.2
  570.9 57.6 %reduce-scatter.37.cloned.1.call-done = bf16[2048,576]{0,1:T(8,128)(2,1)} async-done(((bf16[2048,1152]{0,1:T(8,128)(2,1)}), bf16[2048,576]{0,1:T(8,128)(2,1)}) %reduce-scatter.37.cloned.1.call-update) | async-done | bytes 2359312 | tf_op jit(solution)/shard_map/reduce_scatter | solution.py:50
  628.5 7.4 fusion.150
  636.0 57.2 %all-gather.25.cloned.1.call-done = bf16[2048,1152]{0,1:T(8,128)(2,1)} async-done(((bf16[2048,576]{0,1:T(8,128)(2,1)}), bf16[2048,1152]{0,1:T(8,128)(2,1)}) %all-gather.25.cloned.1.call-update) | async-done | bytes 4718608 | tf_op jit(solution)/shard_map/all_gather | solution.py:56
  693.1 7.2 fusion.172
  700.4 57.4 %all-gather.29.cloned.1.call-done = bf16[2048,1152]{0,1:T(8,128)(2,1)} async-done(((bf16[2048,576]{0,1:T(8,128)(2,1)}), bf16[2048,1152]{0,1:T(8,128)(2,1)}) %all-gather.29.cloned.1.call-update) | async-done | bytes 4718608 | tf_op jit(solution)/shard_map/all_gather | solution.py:56
  757.8 7.2 fusion.173
  765.7 42.4 %reduce-scatter.35.cloned.1.call-done = f32[512,576]{0,1:T(8,128)} async-done(((f32[2048,576]{0,1:T(8,128)}), f32[512,576]{0,1:T(8,128)}) %reduce-scatter.35.cloned.1.call-update) | async-done | bytes 1179664 | tf_op jit(solution)/shard_map/reduce_scatter | solution.py:36
  808.2 50.4 %reduce-scatter.39.cloned.1.call-done = f32[512,576]{0,1:T(8,128)} async-done(((f32[2048,576]{0,1:T(8,128)}), f32[512,576]{0,1:T(8,128)}) %reduce-scatter.39.cloned.1.call-update) | async-done | bytes 1179664 | tf_op jit(solution)/shard_map/reduce_scatter | solution.py:36
  858.6 4.0 fusion.148
  862.5 4.9 all-reduce.1
  870.8 24.2 %all-gather.31.cloned.1.call-done = bf16[2048,576]{0,1:T(8,128)(2,1)} async-done(((bf16[512,576]{0,1:T(8,128)(2,1)}), bf16[2048,576]{0,1:T(8,128)(2,1)}) %all-gather.31.cloned.1.call-update) | async-done | bytes 2359312 | tf_op jit(solution)/shard_map/all_gather | solution.py:32
  895.0 4.2 fusion.174
  899.2 34.8 %reduce-scatter.41.cloned.1.call-done = f32[2048,144]{0,1:T(8,128)} async-done(((f32[2048,288]{0,1:T(8,128)}), f32[2048,144]{0,1:T(8,128)}) %reduce-scatter.41.cloned.1.call-update) | async-done | bytes 1179664 | tf_op jit(solution)/shard_map/reduce_scatter | solution.py:46
  937.7 9.2 while.54
  949.6 22.9 %all-gather.33.cloned.1.call-done = bf16[2048,288]{0,1:T(8,128)(2,1)} async-done(((bf16[2048,144]{0,1:T(8,128)(2,1)}), bf16[2048,288]{0,1:T(8,128)(2,1)}) %all-gather.33.cloned.1.call-update) | async-done | bytes 1179664 | tf_op jit(solution)/shard_map/all_gather | solution.py:42
  972.5 4.8 fusion.162
  977.4 47.9 %reduce-scatter.43.cloned.1.call-done = f32[512,576]{0,1:T(8,128)} async-done(((f32[2048,576]{0,1:T(8,128)}), f32[512,576]{0,1:T(8,128)}) %reduce-scatter.43.cloned.1.call-update) | async-done | bytes 1179664 | tf_op jit(solution)/shard_map/reduce_scatter | solution.py:36
  1029.3 24.0 %all-gather.35.cloned.1.call-done = bf16[2048,576]{0,1:T(8,128)(2,1)} async-done(((bf16[512,576]{0,1:T(8,128)(2,1)}), bf16[2048,576]{0,1:T(8,128)(2,1)}) %all-gather.35.cloned.1.call-update) | async-done | bytes 2359312 | tf_op jit(solution)/shard_map/all_gather | solution.py:32
  1053.3 4.2 fusion.175
  1057.5 34.8 %reduce-scatter.45.cloned.1.call-done = f32[2048,144]{0,1:T(8,128)} async-done(((f32[2048,288]{0,1:T(8,128)}), f32[2048,144]{0,1:T(8,128)}) %reduce-scatter.45.cloned.1.call-update) | async-done | bytes 1179664 | tf_op jit(solution)/shard_map/reduce_scatter | solution.py:46
  1098.8 22.9 %while.55 = (s32[]{:T(128)}, bf16[2,1024,2,72]{1,3,2,0:T(8,128)(2,1)}, bf16[2,1024,2,72]{1,3,2,0:T(8,128)(2,1)}, bf16[2,1024,2,72]{1,3,2,0:T(8,128)(2,1)}, bf16[...) while((s32[]{:T(128)}, ...), condition=%wide.region_40.41_spmd, body=%wide.region_38.40_spmd.sunk | while | flops 1535850496 | bytes 82441536 | solution.py:134
  1126.3 7.5 convolution_convert_fusion.5
  1133.9 6.7 convolution_convert_fusion.6
  1142.2 3.9 convolution_convert_fusion.9
  1146.5 5.0 all_gather.63
  1151.5 5.0 all_gather.62
  1161.2 4.0 convolution_convert_fusion.10
  1172.3 3.8 convolution_convert_fusion.12
  1176.2 21.2 %all-gather.37.cloned.1.call-done = bf16[2048,288]{0,1:T(8,128)(2,1)} async-done(((bf16[2048,144]{0,1:T(8,128)(2,1)}), bf16[2048,288]{0,1:T(8,128)(2,1)}) %all-gather.37.cloned.1.call-update) | async-done | bytes 1179664 | tf_op jit(solution)/shard_map/all_gather | solution.py:283
  1211.4 20.5 %all-reduce.10.cloned.1.call-done = bf16[240,576]{0,1:T(8,128)(2,1)} async-done(((bf16[240,576]{0,1:T(8,128)(2,1)}), bf16[240,576]{0,1:T(8,128)(2,1)}) %all-reduce.10.cloned.1.call-update) | async-done | bytes 276496 | tf_op jit(solution)/shard_map/psum | solution.py:321
  1234.2 206.8 %all-reduce.12.cloned.1.call-done = (bf16[576,288]{0,1:T(8,128)(2,1)}, bf16[576,288]{0,1:T(8,128)(2,1)}, bf16[576,288]{0,1:T(8,128)(2,1)}, bf16[288,576]{1,0:T(8...) async-done(((bf16[576,288]{0,1:T(8,128)(2,1)}, ...) | async-done | bytes 5308432 | tf_op jit(solution)/shard_map/psum | solution.py:331
  1453.9 36.4 %reduce-scatter.47.cloned.1.call-done = f32[512,576]{0,1:T(8,128)} async-done(((f32[2048,576]{0,1:T(8,128)}), f32[512,576]{0,1:T(8,128)}) %reduce-scatter.47.cloned.1.call-update) | async-done | bytes 1179664 | tf_op jit(solution)/shard_map/reduce_scatter | solution.py:36
  1492.3 4.9 all-reduce
  1506.0 10.3 all-reduce.4
  1516.5 19.1 %all-reduce.5 = (bf16[6,576]{1,0:T(8,128)(2,1)S(1)}, bf16[144]{0:T(256)(128)(2,1)S(1)}, bf16[144]{0:T(256)(128)(2,1)S(1)}, bf16[576]{0:T(1024)(128)(2,1)S(1)}, b...) all-reduce(bf16[6,576]{1,0:T(8,128)(2,1)S(1)} %convert_element_type, ...), channel_id=1, replica_groups=mesh['dp'=4,'row'=4,'col'=2] {'dp'}, use_global_device_ids=true, to_apply=%region_49.50 | all-reduce | flops 6336 | bytes 25344 | tf_op jit(solution)/shard_map/psum | solution.py:330
  (431 shorter events, 190.4 us)
Async XLA Ops:
  7.2 496.8 %copy-start = (bf16[1152,576]{0,1:T(8,128)(2,1)S(1)}, bf16[1152,576]{0,1:T(8,128)(2,1)}, u32[]{:S(2)}) copy-start(bf16[1152,576]{0,1:T(8,128)(2,1)} %param.51) | copy-start | bytes 3981316
  7.2 42.0 %all-gather.15.cloned.1.call-start = ((), (), s32[]{:S(2)}) async-start(), calls=%async_computation.16 | async-start | bytes 2949120 | tf_op jit(solution)/shard_map/all_gather | solution.py:32
  7.3 8.9 copy-start.71
  16.2 5.8 copy-start.5
  19.2 30.0 %copy-start.34 = (bf16[576,288]{0,1:T(8,128)(2,1)S(1)}, bf16[576,288]{0,1:T(8,128)(2,1)}, u32[]{:S(2)}) copy-start(bf16[576,288]{0,1:T(8,128)(2,1)} %param.37) | copy-start | bytes 995332
  23.2 65.1 %reduce-scatter.17.cloned.1.call-start = ((), (), s32[]{:S(2)}) async-start(), calls=%async_computation.17 | async-start | bytes 3538944 | tf_op jit(solution)/shard_map/reduce_scatter | solution.py:198
  53.4 72.5 %reduce-scatter.19.cloned.1.call-start = ((), (), s32[]{:S(2)}) async-start(), calls=%async_computation.18 | async-start | bytes 3538944 | tf_op jit(solution)/shard_map/reduce_scatter | solution.py:196
  58.5 104.2 %reduce-scatter.21.cloned.1.call-start = ((), (), s32[]{:S(2)}) async-start(), calls=%async_computation.19 | async-start | bytes 3538944 | tf_op jit(solution)/shard_map/reduce_scatter | solution.py:197
  64.0 140.3 %all-gather.17.cloned.1.call-start = ((), (), s32[]{:S(2)}) async-start(), calls=%async_computation.20 | async-start | bytes 1769472 | tf_op jit(solution)/shard_map/all_gather | solution.py:42
  178.7 25.6 %copy-start.39 = (bf16[288,576]{1,0:T(8,128)(2,1)S(1)}, bf16[288,576]{1,0:T(8,128)(2,1)}, u32[]{:S(2)}) copy-start(bf16[288,576]{1,0:T(8,128)(2,1)} %param.40) | copy-start | bytes 995332
  181.4 75.8 %reduce-scatter.23.cloned.1.call-start = ((), (), s32[]{:S(2)}) async-start(), calls=%async_computation.21 | async-start | bytes 5898240 | tf_op jit(solution)/shard_map/reduce_scatter | solution.py:36
  209.2 50.8 %copy-start.24 = (bf16[240,576]{0,1:T(8,128)(2,1)S(1)}, bf16[240,576]{0,1:T(8,128)(2,1)}, u32[]{:S(2)}) copy-start(bf16[240,576]{0,1:T(8,128)(2,1)} %param.32) | copy-start | bytes 829444
  209.2 74.9 %all-gather.19.cloned.1.call-start = ((), (), s32[]{:S(2)}) async-start(), calls=%async_computation.23 | async-start | bytes 2949120 | tf_op jit(solution)/shard_map/all_gather | solution.py:32
  209.9 52.1 %copy-start.63 = (f32[576]{0:T(1024)}, f32[576]{0:T(1024)S(1)}, u32[]{:S(2)}) copy-start(f32[576]{0:T(1024)S(1)} %convert_element_type.304) | copy-start | bytes 6916
  259.9 24.3 %copy-start.37 = (bf16[576,288]{0,1:T(8,128)(2,1)S(1)}, bf16[576,288]{0,1:T(8,128)(2,1)}, u32[]{:S(2)}) copy-start(bf16[576,288]{0,1:T(8,128)(2,1)} %param.42) | copy-start | bytes 995332
  259.9 39.1 %reduce-scatter.29.cloned.1.call-start = ((), (), s32[]{:S(2)}) async-start(), calls=%async_computation.25 | async-start | bytes 442368 | tf_op jit(solution)/shard_map/reduce_scatter | solution.py:199
  262.0 51.9 %reduce-scatter.25.cloned.1.call-start = ((), (), s32[]{:S(2)}) async-start(), calls=%async_computation.22 | async-start | bytes 442368 | tf_op jit(solution)/shard_map/reduce_scatter | solution.py:200
  264.1 87.2 %reduce-scatter.27.cloned.1.call-start = ((), (), s32[]{:S(2)}) async-start(), calls=%async_computation.24 | async-start | bytes 3538944 | tf_op jit(solution)/shard_map/reduce_scatter | solution.py:46
  288.3 98.2 %all-gather.21.cloned.1.call-start = ((), (), s32[]{:S(2)}) async-start(), calls=%async_computation.26 | async-start | bytes 1769472 | tf_op jit(solution)/shard_map/all_gather | solution.py:42
  360.8 25.7 %copy-start.36 = (bf16[288,576]{1,0:T(8,128)(2,1)S(1)}, bf16[288,576]{1,0:T(8,128)(2,1)}, u32[]{:S(2)}) copy-start(bf16[288,576]{1,0:T(8,128)(2,1)} %param.47) | copy-start | bytes 995332
  363.5 75.8 %reduce-scatter.31.cloned.1.call-start = ((), (), s32[]{:S(2)}) async-start(), calls=%async_computation.27 | async-start | bytes 5898240 | tf_op jit(solution)/shard_map/reduce_scatter | solution.py:36
  391.3 86.6 %all-gather.23.cloned.1.call-start = ((), (), s32[]{:S(2)}) async-start(), calls=%async_computation.28 | async-start | bytes 2949120 | tf_op jit(solution)/shard_map/all_gather | solution.py:32
  453.7 50.3 %all-gather.27.cloned.1.call-start = ((), (), s32[]{:S(2)}) async-start(), calls=%async_computation.32 | async-start | bytes 2949120 | tf_op jit(solution)/shard_map/all_gather | solution.py:32
  456.7 109.5 %reduce-scatter.33.cloned.1.call-start = ((), (), s32[]{:S(2)}) async-start(), calls=%async_computation.29 | async-start | bytes 7077888 | tf_op jit(solution)/shard_map/reduce_scatter | solution.py:50
  486.0 142.5 %reduce-scatter.37.cloned.1.call-start = ((), (), s32[]{:S(2)}) async-start(), calls=%async_computation.33 | async-start | bytes 7077888 | tf_op jit(solution)/shard_map/reduce_scatter | solution.py:50
  511.2 182.0 %all-gather.25.cloned.1.call-start = ((), (), s32[]{:S(2)}) async-start(), calls=%async_computation.30 | async-start | bytes 7077888 | tf_op jit(solution)/shard_map/all_gather | solution.py:56
  570.4 187.3 %all-gather.29.cloned.1.call-start = ((), (), s32[]{:S(2)}) async-start(), calls=%async_computation.34 | async-start | bytes 7077888 | tf_op jit(solution)/shard_map/all_gather | solution.py:56
  635.9 172.3 %reduce-scatter.35.cloned.1.call-start = ((), (), s32[]{:S(2)}) async-start(), calls=%async_computation.31 | async-start | bytes 5898240 | tf_op jit(solution)/shard_map/reduce_scatter | solution.py:36
  700.3 57.5 %copy-start.79 = (bf16[576,1152]{1,0:T(8,128)(2,1)S(1)}, bf16[576,1152]{1,0:T(8,128)(2,1)}, u32[]{:S(2)}) copy-start(bf16[576,1152]{1,0:T(8,128)(2,1)} %param.49) | copy-start | bytes 3981316
  700.4 158.2 %reduce-scatter.39.cloned.1.call-start = ((), (), s32[]{:S(2)}) async-start(), calls=%async_computation.35 | async-start | bytes 5898240 | tf_op jit(solution)/shard_map/reduce_scatter | solution.py:36
  765.0 93.6 %copy-start.3 = (f32[512,576]{0,1:T(8,128)S(1)}, f32[512,576]{0,1:T(8,128)}, u32[]{:S(2)}) copy-start(f32[512,576]{0,1:T(8,128)} %get-tuple-element.412) | copy-start | bytes 3538948
  765.0 93.6 %copy-start.58 = (f32[512,1]{0,1:T(1,128)S(1)}, f32[512,1]{0,1:T(1,128)}, u32[]{:S(2)}) copy-start(f32[512,1]{0,1:T(1,128)} %copy-done.57) | copy-start | bytes 6148
  765.0 93.6 %copy-start.61 = (f32[512,1]{0,1:T(1,128)S(1)}, f32[512,1]{0,1:T(1,128)}, u32[]{:S(2)}) copy-start(f32[512,1]{0,1:T(1,128)} %copy-done.60) | copy-start | bytes 6148
  765.1 129.9 %all-gather.31.cloned.1.call-start = ((), (), s32[]{:S(2)}) async-start(), calls=%async_computation.36 | async-start | bytes 2949120 | tf_op jit(solution)/shard_map/all_gather | solution.py:32
  765.7 96.8 %copy-start.69 = (f32[576]{0:T(1024)}, f32[576]{0:T(1024)S(1)}, u32[]{:S(2)}) copy-start(f32[576]{0:T(1024)S(1)} %convert_element_type.317) | copy-start | bytes 6916
  870.7 63.3 %reduce-scatter.41.cloned.1.call-start = ((), (), s32[]{:S(2)}) async-start(), calls=%async_computation.37 | async-start | bytes 3538944 | tf_op jit(solution)/shard_map/reduce_scatter | solution.py:46
  899.2 73.3 %all-gather.33.cloned.1.call-start = ((), (), s32[]{:S(2)}) async-start(), calls=%async_computation.38 | async-start | bytes 1769472 | tf_op jit(solution)/shard_map/all_gather | solution.py:42
  946.9 30.5 %copy-start.55 = (bf16[2,120,2,72]{1,3,2,0:T(8,128)(2,1)}, bf16[2,120,2,72]{1,3,2,0:T(8,128)(2,1)S(1)}, u32[]{:S(2)}) copy-start(bf16[2,120,2,72]{1,3,2,0:T(8,128)(2,1)S(1)} %get-tuple-element.195) | copy-start | bytes 207364
  946.9 25.6 %copy-start.38 = (bf16[576,288]{0,1:T(8,128)(2,1)S(1)}, bf16[576,288]{0,1:T(8,128)(2,1)}, u32[]{:S(2)}) copy-start(bf16[576,288]{0,1:T(8,128)(2,1)} %param.42) | copy-start | bytes 995332
  949.6 75.8 %reduce-scatter.43.cloned.1.call-start = ((), (), s32[]{:S(2)}) async-start(), calls=%async_computation.39 | async-start | bytes 5898240 | tf_op jit(solution)/shard_map/reduce_scatter | solution.py:36
  977.3 48.0 %copy-start.4 = (f32[512,576]{0,1:T(8,128)S(1)}, f32[512,576]{0,1:T(8,128)}, u32[]{:S(2)}) copy-start(f32[512,576]{0,1:T(8,128)} %get-tuple-element.412) | copy-start | bytes 3538948
  977.4 48.0 %copy-start.11 = (bf16[512,576]{0,1:T(8,128)(2,1)S(1)}, bf16[512,576]{0,1:T(8,128)(2,1)}, u32[]{:S(2)}) copy-start(bf16[512,576]{0,1:T(8,128)(2,1)} %param.53) | copy-start | bytes 1769476
  977.4 75.9 %copy-start.40 = (bf16[288,576]{1,0:T(8,128)(2,1)S(1)}, bf16[288,576]{1,0:T(8,128)(2,1)}, u32[]{:S(2)}) copy-start(bf16[288,576]{1,0:T(8,128)(2,1)} %param.40) | copy-start | bytes 995332
  977.4 75.9 %all-gather.35.cloned.1.call-start = ((), (), s32[]{:S(2)}) async-start(), calls=%async_computation.40 | async-start | bytes 2949120 | tf_op jit(solution)/shard_map/all_gather | solution.py:32
  1029.1 63.3 %reduce-scatter.45.cloned.1.call-start = ((), (), s32[]{:S(2)}) async-start(), calls=%async_computation.41 | async-start | bytes 3538944 | tf_op jit(solution)/shard_map/reduce_scatter | solution.py:46
  1057.5 109.6 %all-gather.39.cloned.1.call-start = ((), (), s32[]{:S(2)}) async-start(), calls=%async_computation.43 | async-start | bytes 1769472 | tf_op jit(solution)/shard_map/all_gather | solution.py:284
  1124.4 48.0 %all-gather.41.cloned.1.call-start = ((), (), s32[]{:S(2)}) async-start(), calls=%async_computation.44 | async-start | bytes 1769472 | tf_op jit(solution)/shard_map/all_gather | solution.py:285
  1126.0 71.3 %all-gather.37.cloned.1.call-start = ((), (), s32[]{:S(2)}) async-start(), calls=%async_computation.42 | async-start | bytes 1769472 | tf_op jit(solution)/shard_map/all_gather | solution.py:283
  1126.3 7.6 copy-start.78
  1133.9 6.7 copy-start.23
  1142.2 14.4 copy-start.25
  1142.2 89.7 %all-reduce.10.cloned.1.call-start = ((), (), s32[]{:S(2)}) async-start(), calls=%async_computation.46 | async-start | bytes 589824 | tf_op jit(solution)/shard_map/psum | solution.py:321
  1146.2 12.5 copy-start.45
  1161.1 279.9 %all-reduce.12.cloned.1.call-start = ((), (), s32[]{:S(2)}) async-start(), calls=%async_computation.47 | async-start | bytes 11206656 | tf_op jit(solution)/shard_map/psum | solution.py:331
  1161.2 4.0 copy-start.27
  1161.2 4.0 copy-start.33
  1201.2 289.1 %reduce-scatter.47.cloned.1.call-start = ((), (), s32[]{:S(2)}) async-start(), calls=%async_computation.45 | async-start | bytes 5898240 | tf_op jit(solution)/shard_map/reduce_scatter | solution.py:36
  1441.0 4.9 copy-start.53
  1441.0 5.8 copy-start.52
  1443.0 4.7 copy-start.51
  1452.1 38.2 %copy-start.6 = (bf16[512,576]{0,1:T(8,128)(2,1)S(1)}, bf16[512,576]{0,1:T(8,128)(2,1)}, u32[]{:S(2)}) copy-start(bf16[512,576]{0,1:T(8,128)(2,1)} %param.31) | copy-start | bytes 1769476
  1452.2 38.2 %copy-start.66 = (f32[512,1]{0,1:T(1,128)S(1)}, f32[512,1]{0,1:T(1,128)}, u32[]{:S(2)}) copy-start(f32[512,1]{0,1:T(1,128)} %copy-done.65) | copy-start | bytes 6148
  1452.2 38.2 %copy-start.68 = (f32[512,1]{0,1:T(1,128)S(1)}, f32[512,1]{0,1:T(1,128)}, u32[]{:S(2)}) copy-start(f32[512,1]{0,1:T(1,128)} %copy-done.67) | copy-start | bytes 6148
  1502.7 13.8 copy-start.73
  (64 other events, 112.4 us)
Sparse Core Ops, SparseCore 0:
  23.3 25.8 all-gather.14
  53.5 34.7 reduce-scatter.16
  91.2 34.6 reduce-scatter.18
  128.0 34.7 reduce-scatter.20
  181.5 22.7 all-gather.16
  209.3 47.8 reduce-scatter.22
  260.0 24.0 all-gather.18
  286.9 12.0 reduce-scatter.28
  301.8 12.0 reduce-scatter.24
  316.6 34.6 reduce-scatter.26
  363.6 22.7 all-gather.20
  391.5 47.7 reduce-scatter.30
  453.8 24.0 all-gather.22
  479.9 24.0 all-gather.26
  506.2 59.9 reduce-scatter.32
  568.5 59.9 reduce-scatter.36
  630.4 62.6 all-gather.24
  695.1 62.6 all-gather.28
  760.3 47.8 reduce-scatter.34
  810.7 47.8 reduce-scatter.38
  870.8 24.0 all-gather.30
  899.3 34.7 reduce-scatter.40
  949.7 22.7 all-gather.32
  977.5 47.7 reduce-scatter.42
  1029.2 24.0 all-gather.34
  1057.6 34.7 reduce-scatter.44
  1124.5 22.7 all-gather.38
  1149.5 22.7 all-gather.40
  1174.5 22.7 all-gather.36
  1199.6 32.1 all-reduce.9
  1237.1 203.8 all-reduce.11
  1443.7 46.5 reduce-scatter.46
where the time goes:
time: 1560 us; the launch traced here: 1550 us
  waiting for transfers between devices  1170 us (75%)
  matrix products  160 us (10%)
  other arithmetic  89.8 us (6%)
  blocking collectives  60.7 us (4%)
  local copies, waits for them, and re-layouts  51.4 us (3%)
    reduce_scatter x6, waiting for transfers between devices, rows_out(): lax.psum_scatter(terms(jnp.int32(0), tok_rows * lax.axis_size('row')), 'r...  271 us
    psum x1, waiting for transfers between devices, on_device(): lax.psum(q_weight_grad.astype(jnp.bfloat16), 'dp').astype(jnp.float32)  207 us
    all_gather x6, waiting for transfers between devices, rows_in(): return lax.all_gather(value, 'row', axis=0, tiled=True)  133 us
    all_gather x2, waiting for transfers between devices, hidden_in(): return lax.all_gather(value, 'col', axis=1, tiled=True)  115 us
    reduce_scatter x2, waiting for transfers between devices, hidden_sums(): lax.psum_scatter(value.astype(jnp.bfloat16), 'col', scatter_dimension=1,...  111 us
    reduce_scatter x3, waiting for transfers between devices, head_sums(): return lax.psum_scatter(value, 'col', scatter_dimension=1, tiled=True)  105 us
    all_gather x3, waiting for transfers between devices, heads_in(): return lax.all_gather(value, 'col', axis=1, tiled=True)  68.7 us
    dot_general x10, matrix products, plain_dot(): return jnp.dot(left, right, preferred_element_type=FLOAT)  45.8 us
  transfers between devices with their start and end apart: 32, of which 31 were waited for; matrix products, arithmetic and copies ran while one was open for 9% of the time, Pallas kernels for 0%

commit v1 on v0

v1 whole, which is shorter than its diff:
```python
import jax
import jax.numpy as jnp
from jax import lax
from jax.experimental import pallas as pl
from jax.experimental.pallas import tpu as pltpu
from jax.sharding import PartitionSpec as P


D = 1152
HD = 72
FLOAT = jnp.float32
HALF = jnp.bfloat16
EPSILON = 1e-06
SCALE = HD ** (-0.5)
VMEM_BYTES = 48 * 1024 * 1024

CORE = [(i, i ^ 1) for i in range(4)]
ACROSS = [(i, i ^ 2) for i in range(4)]
SWAP = [(0, 1), (1, 0)]


def place(x, k, y):
    return (x * 2 + k) * 2 + y


POINTS = [(x, k, y) for x in range(2) for k in range(2) for y in range(2)]
TURN = [(place(x, k, y), place(y, k, x)) for x, k, y in POINTS]
TURN_IN = [(place(x, k, y), place(1 - y, k, x)) for x, k, y in POINTS]
TURN_OUT = [(place(x, k, y), place(y, k, 1 - x)) for x, k, y in POINTS]


def to_core(value):
    return lax.ppermute(value, "row", CORE)


def to_x(value):
    return lax.ppermute(value, "row", ACROSS)


def to_y(value):
    return lax.ppermute(value, "col", SWAP)


def tie(*values):
    return lax.optimization_barrier(values)


def dot(left, right):
    return jnp.dot(left, right, preferred_element_type=FLOAT)


def lead_dot(left, right):
    return lax.dot_general(left, right, (((0,), (0,)), ((), ())), preferred_element_type=FLOAT)


def tail_dot(left, right):
    return lax.dot_general(left, right, (((1,), (1,)), ((), ())), preferred_element_type=FLOAT)


def cat(parts, axis):
    return jnp.concatenate(parts, axis)


def half(value):
    return value.astype(HALF)


def wide(value):
    return value.astype(FLOAT)


def tokens_sent(value, y):
    mid = value.shape[0] // 2
    low, high = value[:mid], value[mid:]
    first = lax.ppermute(jnp.where(y == 0, low, high), ("row", "col"), TURN)
    return first, lax.ppermute(jnp.where(y == 0, high, low), ("row", "col"), TURN_IN)


def tokens_got(first, second, same):
    return cat((jnp.where(same, first, second), jnp.where(same, second, first)), 1)


def halves_sent(pair, same):
    mid = pair.shape[1] // 2
    low, high = pair[:, :mid], pair[:, mid:]
    first = lax.ppermute(jnp.where(same, low, high), ("row", "col"), TURN)
    return first, lax.ppermute(jnp.where(same, high, low), ("row", "col"), TURN_OUT)


def halves_got(first, second, y):
    return cat((jnp.where(y == 0, first, second), jnp.where(y == 0, second, first)), 0)


def pair_mean(pair):
    return (jnp.sum(pair[0], 1, keepdims=True) + jnp.sum(pair[1], 1, keepdims=True)) / D


def layer_norm(pair):
    average = pair_mean(pair)
    center = [v - average for v in pair]
    inv_std = lax.rsqrt(pair_mean([c * c for c in center]) + EPSILON)
    return [c * inv_std for c in center], inv_std


def layer_norm_back(grad, normed, inv_std):
    average = pair_mean(grad)
    crossed = pair_mean([g * n for g, n in zip(grad, normed)])
    return [inv_std * (g - average - n * crossed) for g, n in zip(grad, normed)]


def row_sum(value):
    return jnp.sum(value, 0, keepdims=True)


def gelu(v):
    return 0.5 * v * (1.0 + jnp.tanh(0.7978845608028654 * (v + 0.044715 * v * v * v)))


def gelu_slope(v):
    t = jnp.tanh(0.7978845608028654 * (v + 0.044715 * v * v * v))
    return 0.5 * (1.0 + t) + 0.5 * v * (1.0 - t * t) * 0.7978845608028654 * (
        1.0 + 3.0 * 0.044715 * v * v
    )


def call(kernel, outs, args, scratch=(), smem=()):
    vmem = pl.BlockSpec(memory_space=pltpu.VMEM)
    specs = [pl.BlockSpec(memory_space=pltpu.SMEM) if i in smem else vmem for i in range(len(args))]
    return pl.pallas_call(
        kernel,
        out_shape=outs,
        in_specs=specs,
        out_specs=[vmem] * len(outs),
        scratch_shapes=scratch,
        compiler_params=pltpu.CompilerParams(vmem_limit_bytes=VMEM_BYTES),
        cost_estimate=pl.CostEstimate(flops=1, bytes_accessed=1, transcendentals=0),
    )(*args)


class Pair:
    def __init__(self, ref, count=2):
        self.ref, self.size, self.rows = ref, ref.shape[1] // count, ref.shape[0]

    def __getitem__(self, i):
        return self.ref[:, pl.ds(i * self.size, self.size)]

    def __setitem__(self, i, value):
        self.ref[:, pl.ds(i * self.size, self.size)] = value


def shape(dims, dtype):
    return jax.ShapeDtypeStruct(dims, dtype)


def bias_kernel(first_col, own, got, out):
    quarter = own.shape[1] // 4
    low_own = first_col[0] == 1
    at = 0
    for r, begin, size in [(0, i * quarter, quarter) for i in range(4)] + [(1, 0, 4 * quarter)]:
        a, b = own[r : r + 1, pl.ds(begin, size)], got[r : r + 1, pl.ds(begin, size)]
        out[:, pl.ds(at, size)] = jnp.where(low_own, a, b)
        out[:, pl.ds(at + size, size)] = jnp.where(low_own, b, a)
        at += 2 * size


def norm_kernel(x_ref, mods, out):
    x_ref, out = Pair(x_ref), Pair(out)
    normed, _ = layer_norm([wide(x_ref[0]), wide(x_ref[1])])
    for i in range(2):
        out[i] = half(normed[i] * (1.0 + mods[i, 1:2, :]) + mods[i, 0:1, :])


def project_kernel(near, far, own_m, got_m, own_s, got_s, row_m, row_s, q_out, kv_out):
    near, far = Pair(near), Pair(far)
    own_m, got_m, own_s, got_s = (Pair(w, 3) for w in (own_m, got_m, own_s, got_s))
    block = own_m.rows
    rows = near.rows
    for part in range(2):
        a, b = (near, far)[part][0], (near, far)[part][1]
        at = pl.ds(part * rows, rows)
        for i in range(3):
            for j in range(2):
                own, got = ((own_m, got_m), (own_s, got_s))[j]
                bias = (row_m, row_s)[j]
                out = tail_dot(a, own[i]) + tail_dot(b, got[i])
                if i == 0:
                    q_out[at, pl.ds(j * block, block)] = half(out + bias[:, :block])
                else:
                    if i == 2:
                        out = out + bias[:, block : 2 * block]
                    kv_out[at, pl.ds(((i - 1) * 2 + j) * block, block)] = half(out)


def attend_head(q, k, v):
    scores = tail_dot(k, q) * SCALE
    peak = jnp.max(scores, 0, keepdims=True)
    raised = jnp.exp(scores - peak)
    summed = jnp.sum(raised, 0, keepdims=True)
    mixed = dot(v.T, half(raised)) / summed
    return half(mixed.T), peak + jnp.log(summed)


def attend_head_back(q, k, v, g, lse):
    prob = jnp.exp(tail_dot(k, q) * SCALE - lse)
    grad_prob = tail_dot(v, g)
    centre = jnp.sum(prob * grad_prob, 0, keepdims=True)
    grad_score = half(prob * (grad_prob - centre))
    grad_q = (dot(k.T, grad_score) * SCALE).T
    grad_k = dot(grad_score, q) * SCALE
    grad_v = dot(half(prob), g)
    return grad_q, grad_k, grad_v


def attend_kernel(q_ref, near, far, out_ref, lse_ref):
    heads = q_ref.shape[1] // HD
    width = heads * HD
    for h in range(heads):
        at = pl.ds(h * HD, HD)
        there = (h + heads // 2) % heads * HD
        k = cat((near[:, at], far[:, pl.ds(there, HD)]), 0)
        v = cat((near[:, pl.ds(width + h * HD, HD)], far[:, pl.ds(width + there, HD)]), 0)
        for c in range(2):
            rows = pl.ds(c * (q_ref.shape[0] // 2), q_ref.shape[0] // 2)
            mixed, lse = attend_head(q_ref[rows, at], k, v)
            out_ref[rows, at] = mixed
            lse_ref[pl.ds(h, 1), rows] = lse


def attend_back_kernel(q_ref, near, far, lse_ref, g_ref, gq_ref, keep_ref, send_ref):
    heads = q_ref.shape[1] // HD
    width = heads * HD
    tokens = near.shape[0]
    for h in range(heads):
        at = pl.ds(h * HD, HD)
        there = (h + heads // 2) % heads * HD
        k = cat((near[:, at], far[:, pl.ds(there, HD)]), 0)
        v = cat((near[:, pl.ds(width + h * HD, HD)], far[:, pl.ds(width + there, HD)]), 0)
        total_k, total_v = None, None
        for c in range(2):
            rows = pl.ds(c * (q_ref.shape[0] // 2), q_ref.shape[0] // 2)
            gq, gk, gv = attend_head_back(
                q_ref[rows, at], k, v, g_ref[rows, at], lse_ref[pl.ds(h, 1), rows]
            )
            gq_ref[rows, at] = half(gq)
            total_k = gk if total_k is None else total_k + gk
            total_v = gv if total_v is None else total_v + gv
        keep_ref[:, at] = total_k[:tokens]
        keep_ref[:, pl.ds(width + h * HD, HD)] = total_v[:tokens]
        send_ref[:, pl.ds(there, HD)] = half(total_k[tokens:])
        send_ref[:, pl.ds(width + there, HD)] = half(total_v[tokens:])


def out_kernel(att, own_m, got_m, own_s, got_s, near, far):
    near, far = Pair(near), Pair(far)
    block = own_m.shape[0]
    rows = near.rows
    for part in range(2):
        at = pl.ds(part * rows, rows)
        a, b = att[at, :block], att[at, pl.ds(block, block)]
        for i in range(2):
            w_m, w_s = ((own_m, own_s), (got_m, got_s))[i]
            out = dot(a, w_m[...]) + dot(b, w_s[...])
            if part == 0:
                near[i] = out
            else:
                far[i] = half(out)


def out_back_kernel(near, far, att, own_m, got_m, own_s, got_s, grad_att, keep, send):
    near, far, keep, send = Pair(near), Pair(far), Pair(keep), Pair(send)
    block = own_m.shape[0]
    rows = near.rows
    for part in range(2):
        at = pl.ds(part * rows, rows)
        a, b = (near, far)[part][0], (near, far)[part][1]
        for j in range(2):
            own, got = ((own_m, got_m), (own_s, got_s))[j]
            grad_att[at, pl.ds(j * block, block)] = half(tail_dot(a, own[...]) + tail_dot(b, got[...]))
    for j in range(2):
        a = att[:rows, pl.ds(j * block, block)]
        b = att[rows:, pl.ds(j * block, block)]
        for i in range(2):
            (keep, send)[j][i] = half(lead_dot(a, near[i]) + lead_dot(b, far[i]))


def cross_kernel(x_ref, mods, near, far, row_m, row_s, far_bias, text_near, text_far, *refs):
    weights = [Pair(w) for w in refs[:8]]
    x_ref, near, far = Pair(x_ref), Pair(near), Pair(far)
    attn_out, cross_in, q_out, att_out, lse_ref, two_ref, h_ref = refs[8:]
    attn_out, cross_in, two_ref, h_ref = (Pair(v) for v in (attn_out, cross_in, two_ref, h_ref))
    block = weights[0].rows
    for i in range(2):
        attn = near[i] + wide(far[i]) + mods[i, 6:7, :]
        attn_out[i] = attn
        one = wide(x_ref[i]) + mods[i, 2:3, :] * attn
        cross_in[i] = half(one)
        two_ref[i] = one + mods[i, 7:8, :]
    a, b = cross_in[0], cross_in[1]
    for n in range(4):
        pair = weights[2 * n], weights[2 * n + 1]
        bias = (row_m, row_s)[n][:, 2 * block : 3 * block] if n < 2 else far_bias[:, (n - 2) * block : (n - 1) * block]
        q_out[n] = half(tail_dot(a, pair[0][0]) + tail_dot(b, pair[1][0]) + bias)
        text = (text_near, text_far)[n // 2]
        base = (n % 2) * 2 * block
        for h in range(block // HD):
            at = pl.ds(h * HD, HD)
            mixed, lse = attend_head(
                q_out[n, :, at],
                text[:, pl.ds(base + h * HD, HD)],
                text[:, pl.ds(base + block + h * HD, HD)],
            )
            att_out[n, :, at] = mixed
            lse_ref[pl.ds(n * (block // HD) + h, 1), :] = lse
        att = att_out[n]
        for i in range(2):
            two_ref[i] += dot(att, pair[i][1])
    normed, _ = layer_norm([two_ref[0], two_ref[1]])
    for i in range(2):
        h_ref[i] = half(normed[i] * (1.0 + mods[i, 4:5, :]) + mods[i, 3:4, :])


def cross_back_kernel(g_ref, mods, two_ref, near, far, attn_out, q_ref, lse_ref, text_near, text_far, *refs):
    weights = [Pair(w) for w in refs[:8]]
    g_ref, two_ref, near, far, attn_out = (Pair(v) for v in (g_ref, two_ref, near, far, attn_out))
    grad_cross, gq_out, near_out, far_out, one_ref, grad_attn, sums, grad_scratch = refs[8:]
    grad_cross, one_ref, grad_attn = Pair(grad_cross), Pair(one_ref), Pair(grad_attn)
    block = weights[0].rows
    normed, inv_std = layer_norm([two_ref[0], two_ref[1]])
    grads = [near[i] + wide(far[i]) for i in range(2)]
    back = layer_norm_back([grads[i] * (1.0 + mods[i, 4:5, :]) for i in range(2)], normed, inv_std)
    for i in range(2):
        sums[i, 0:1, :] = row_sum(grads[i])
        sums[i, 1:2, :] = row_sum(grads[i] * normed[i])
        grad = wide(g_ref[i]) + back[i]
        one_ref[i] = grad
        grad_cross[i] = half(grad)
        sums[i, 2:3, :] = row_sum(wide(half(grad)))
    a, b = grad_cross[0], grad_cross[1]
    for n in range(4):
        pair = weights[2 * n], weights[2 * n + 1]
        grad_scratch[...] = half(tail_dot(a, pair[0][1]) + tail_dot(b, pair[1][1]))
        text, text_out = ((text_near, near_out), (text_far, far_out))[n // 2]
        base = (n % 2) * 2 * block
        for h in range(block // HD):
            at = pl.ds(h * HD, HD)
            k_at, v_at = pl.ds(base + h * HD, HD), pl.ds(base + block + h * HD, HD)
            gq, gk, gv = attend_head_back(
                q_ref[n, :, at],
                text[:, k_at],
                text[:, v_at],
                grad_scratch[:, at],
                lse_ref[pl.ds(n * (block // HD) + h, 1), :],
            )
            gq_out[n, :, at] = half(gq)
            text_out[:, k_at] = half(gk)
            text_out[:, v_at] = half(gv)
        gq = gq_out[n]
        for i in range(2):
            one_ref[i] += dot(gq, pair[i][0])
    for i in range(2):
        one = one_ref[i]
        attn = half(one * mods[i, 2:3, :])
        grad_attn[i] = attn
        sums[i, 3:4, :] = row_sum(one * attn_out[i])
        sums[i, 4:5, :] = row_sum(wide(attn))


def cross_weight_kernel(x_ref, g_ref, q_ref, att_ref, keep_m, keep_x, send_m, send_x):
    x_ref, g_ref = Pair(x_ref), Pair(g_ref)
    for n, out in enumerate((keep_m, send_m, keep_x, send_x)):
        out = Pair(out, 4)
        for i in range(2):
            out[2 * i] = half(lead_dot(q_ref[n], x_ref[i]))
            out[2 * i + 1] = half(lead_dot(att_ref[n], g_ref[i]))


def rest_kernel(cqo, cqo_got, text_near, text_got, text_own, text_other, ckv_own, ckv_got, o_ref, o_got, *refs):
    outs, (grad_text, text_part, cv_sum) = refs[:2], refs[2:]
    cqo, cqo_got, o_ref, o_got, text_part = (
        Pair(cqo, 4), Pair(cqo_got, 4), Pair(o_ref), Pair(o_got), Pair(text_part)
    )
    grad_text[...] = half(wide(text_near[...]) + wide(text_got[...]))
    block = cqo.rows
    gk, gv = grad_text[:, :block], grad_text[:, pl.ds(block, block)]
    cv_sum[...] = row_sum(wide(gv))
    for i in range(2):
        out, text, weight = Pair(outs[i], 5), (text_own, text_other)[i], Pair((ckv_own, ckv_got)[i])
        for n in range(2):
            out[n] = half(wide(cqo[2 * i + n]) + wide(cqo_got[2 * i + n]))
        out[2] = half(lead_dot(gk, text[...]))
        out[3] = half(lead_dot(gv, text[...]))
        out[4] = half(wide(o_ref[i]) + wide(o_got[i]))
        text_part[i] = half(dot(gk, weight[0]) + dot(gv, weight[1]))


def up_kernel(near, far, own_m, got_m, own_s, got_s, row_m, row_s, pre, hidden):
    near, far = Pair(near), Pair(far)
    rows, ff = near.rows, own_m.shape[1]
    for part in range(2):
        a, b = (near, far)[part][0], (near, far)[part][1]
        at = pl.ds(part * rows, rows)
        for j in range(2):
            own, got = ((own_m, got_m), (own_s, got_s))[j]
            bias = (row_m, row_s)[j]
            out = dot(a, own[...]) + dot(b, got[...]) + bias[:, pl.ds(bias.shape[1] - ff, ff)]
            pre[j, at, :] = out
            hidden[j, at, :] = half(gelu(out))


def mlp_back_kernel(g_near, g_far, pre, *refs):
    g_near, g_far = Pair(g_near), Pair(g_far)
    up, down, (grad_pre, near, far, sums) = refs[:4], refs[4:8], refs[8:]
    near, far = Pair(near), Pair(far)
    rows = near.rows
    total = [None, None]
    for part in range(2):
        a, b = (g_near, g_far)[part][0], (g_near, g_far)[part][1]
        at = pl.ds(part * rows, rows)
        for j in range(2):
            grad = dot(a, down[2 * j][...]) + dot(b, down[2 * j + 1][...])
            grad = half(grad * gelu_slope(pre[j, at, :]))
            grad_pre[j, at, :] = grad
            term = row_sum(wide(grad))
            total[j] = term if part == 0 else total[j] + term
        for i in range(2):
            out = tail_dot(grad_pre[0, at, :], up[i][...]) + tail_dot(grad_pre[1, at, :], up[2 + i][...])
            if part == 0:
                near[i] = out
            else:
                far[i] = half(out)
    sums[0:1, :] = total[0]
    sums[1:2, :] = total[1]


def ff_weight_kernel(near, far, ff, keep0, keep1, send0, send1):
    near, far = Pair(near), Pair(far)
    rows = near.rows
    for j in range(2):
        for i in range(2):
            out = lead_dot(near[i], ff[j, :rows, :]) + lead_dot(far[i], ff[j, rows:, :])
            ((keep0, keep1), (send0, send1))[j][i][...] = half(out)


def down_kernel(hidden, own_m, got_m, own_s, got_s, near, far):
    near, far = Pair(near), Pair(far)
    rows = near.rows
    for part in range(2):
        at = pl.ds(part * rows, rows)
        for i in range(2):
            w_m, w_s = ((own_m, own_s), (got_m, got_s))[i]
            out = tail_dot(hidden[0, at, :], w_m[...]) + tail_dot(hidden[1, at, :], w_s[...])
            if part == 0:
                near[i] = out
            else:
                far[i] = half(out)


def layer_out_kernel(near, far, two_ref, mods, g_ref, gm_ref, out, sums):
    near, far, two_ref, g_ref, gm_ref, out = (Pair(v) for v in (near, far, two_ref, g_ref, gm_ref, out))
    for i in range(2):
        mlp_out = near[i] + wide(far[i]) + mods[i, 8:9, :]
        out[i] = half(two_ref[i] + mods[i, 5:6, :] * mlp_out)
        sums[i, 0:1, :] = row_sum(wide(g_ref[i]) * mlp_out)
        sums[i, 1:2, :] = row_sum(wide(gm_ref[i]))


def project_back_kernel(gq, keep, got, own_m, got_m, own_s, got_s, near, far, grad_m, grad_s, sums):
    near, far = Pair(near), Pair(far)
    own_m, got_m, own_s, got_s = (Pair(w, 3) for w in (own_m, got_m, own_s, got_s))
    block = own_m.rows
    rows = near.rows
    for part in range(2):
        at = pl.ds(part * rows, rows)
        total = [None, None]
        for i in range(3):
            for j in range(2):
                if i == 0:
                    g = gq[at, pl.ds(j * block, block)]
                else:
                    lanes = pl.ds(((i - 1) * 2 + j) * block, block)
                    g = half(keep[at, lanes] + wide(got[at, lanes]))
                (grad_m, grad_s)[j][at, pl.ds(i * block, block)] = g
                for n in range(2):
                    w = ((own_m, got_m), (own_s, got_s))[j][n]
                    term = dot(g, w[i])
                    total[n] = term if total[n] is None else total[n] + term
        for n in range(2):
            if part == 0:
                near[n] = total[n]
            else:
                far[n] = half(total[n])
    sums[0:1, :] = row_sum(wide(grad_m[...]))
    sums[1:2, :] = row_sum(wide(grad_s[...]))


def project_weight_kernel(near, far, grad_m, grad_s, keep0, keep1, send0, send1):
    near, far = Pair(near), Pair(far)
    rows = near.rows
    for j in range(2):
        grad = (grad_m, grad_s)[j]
        block = grad.shape[1] // 3
        for i in range(2):
            out = Pair(((keep0, keep1), (send0, send1))[j][i], 3)
            for n in range(3):
                g_near = grad[:rows, pl.ds(n * block, block)]
                g_far = grad[rows:, pl.ds(n * block, block)]
                out[n] = half(lead_dot(g_near, near[i]) + lead_dot(g_far, far[i]))


def norm_back_kernel(x_ref, mods, near, far, one_ref, out, sums):
    x_ref, near, far, one_ref, out = (Pair(v) for v in (x_ref, near, far, one_ref, out))
    normed, inv_std = layer_norm([wide(x_ref[0]), wide(x_ref[1])])
    grads = [near[i] + wide(far[i]) for i in range(2)]
    back = layer_norm_back([grads[i] * (1.0 + mods[i, 1:2, :]) for i in range(2)], normed, inv_std)
    for i in range(2):
        out[i] = half(one_ref[i] + back[i])
        sums[i, 0:1, :] = row_sum(grads[i])
        sums[i, 1:2, :] = row_sum(grads[i] * normed[i])


def dp_pairs(step):
    return [(i, i ^ step) for i in range(lax.axis_size("dp"))]


def by_halves(value):
    count = lax.axis_size("dp")
    return count & (count - 1) == 0 and value.shape[0] % count == 0


def dp_steps():
    return [1 << i for i in range(lax.axis_size("dp").bit_length() - 1)]


def reduce_sent(value, step):
    mid = value.shape[0] // 2
    upper = (lax.axis_index("dp") & step) != 0
    low, high = value[:mid], value[mid:]
    got = lax.ppermute(jnp.where(upper, low, high), "dp", dp_pairs(step))
    return jnp.where(upper, high, low), got


def reduce_got(kept, got):
    return half(wide(kept) + wide(got))


def gather_sent(value, step):
    return value, lax.ppermute(value, "dp", dp_pairs(step))


def gather_got(value, got, step):
    upper = (lax.axis_index("dp") & step) != 0
    return cat((jnp.where(upper, got, value), jnp.where(upper, value, got)), 0)


class DpSum:
    def __init__(self, value):
        self.value, self.flying = value, ()
        if by_halves(value):
            self.todo = [(True, step) for step in dp_steps()]
            self.todo += [(False, step) for step in reversed(dp_steps())]
        else:
            self.todo = []
            self.value = lax.psum(value, "dp")

    def send(self):
        if self.todo:
            reduce, step = self.todo[0]
            self.flying = (reduce_sent if reduce else gather_sent)(self.value, step)

    def land(self):
        if self.flying:
            reduce, step = self.todo.pop(0)
            if reduce:
                self.value = reduce_got(*self.flying)
            else:
                self.value = gather_got(*self.flying, step)
            self.flying = ()

    def next(self):
        self.land()
        self.send()

    def finish(self):
        self.land()
        while self.todo:
            self.send()
            self.land()
        return self.value


def tie_sums(sums, *values):
    flying = [v for one in sums for v in one.flying]
    out = tie(*values, *flying)
    rest = list(out[len(values) :])
    for one in sums:
        one.flying = tuple(rest.pop(0) for _ in one.flying)
        one.land()
    return out[: len(values)]


def small_sum_over_dp(value):
    if lax.axis_size("dp") != 4:
        return lax.psum(value, "dp")
    return value + sum(lax.ppermute(value, "dp", dp_pairs(i)) for i in range(1, 4))


def on_device(
    latents_in,
    text_emb,
    time_emb,
    shift_table,
    q_weight,
    k_weight,
    v_weight,
    q_bias,
    v_bias,
    o_weight,
    o_bias,
    cq_weight,
    cq_bias,
    ck_weight,
    cv_weight,
    cv_bias,
    co_weight,
    co_bias,
    up_weight,
    up_bias,
    down_weight,
    down_bias,
    cotangent,
):
    row = lax.axis_index("row")
    y = lax.axis_index("col")
    same = row // 2 == y
    first_col = y == 0
    part = D // 2
    text_rows = text_emb.shape[0] // 2
    block = q_weight.shape[1]
    quarter = block // 2
    ff = up_weight.shape[1]
    own = latents_in.shape[0] // 2
    tokens = 2 * own
    pair_wide, pair_half = shape((own, D), FLOAT), shape((own, D), HALF)

    def in_order(mine, other):
        return jnp.where(first_col, cat((mine, other), 0), cat((other, mine), 0))

    latents = tokens_got(*tokens_sent(latents_in, y), same)
    mods = wide(shift_table)[None] + wide(time_emb)
    row_own = cat((wide(cat((q_bias, v_bias, cq_bias, cv_bias), 0))[None], wide(up_bias)[None]), 0)
    out_bias = jnp.stack([wide(v) for v in (o_bias, co_bias, down_bias)])
    small_got = to_y(cat((jnp.where(first_col, mods[1], mods[0]), out_bias, row_own), 0))
    qkv_own, small_got = tie(cat((q_weight.T, k_weight.T, v_weight.T), 1), small_got)
    mods = jnp.stack((cat((jnp.where(first_col, mods[0], mods[1]), out_bias), 0), small_got[:9]))
    (row_m,) = call(
        bias_kernel,
        [shape((1, 4 * block + ff), FLOAT)],
        [first_col.astype(jnp.int32).reshape(1), row_own, small_got[9:]],
        smem=(0,),
    )
    row_s = to_core(row_m)

    qkv_got = to_y(qkv_own)
    qkv_core = to_core(qkv_own)
    o_core = to_core(o_weight)
    down_own = down_weight.T
    up_core, down_core = to_core(up_weight), to_core(down_own)
    text_own = jnp.where(first_col, text_emb[:text_rows], text_emb[text_rows:])
    text_sent = jnp.where(first_col, text_emb[text_rows:], text_emb[:text_rows])
    o_own, up_own = o_weight, up_weight
    cqo_own, ckv_own = cat((cq_weight.T, co_weight), 1), cat((ck_weight.T, cv_weight.T), 1)
    latents, cqo_own, ckv_own = tie(latents, cqo_own, ckv_own)
    o_got = to_y(o_own)
    cqo_got = to_y(cqo_own)
    (h_one,) = call(norm_kernel, [pair_half], [latents, mods])
    h_one_far = to_x(h_one)

    h_one_far, qkv_got, cqo_own, ckv_own = tie(h_one_far, qkv_got, cqo_own, ckv_own)
    cqo_x = to_x(cqo_own)
    ckv_got = to_y(ckv_own)
    text_got = to_y(text_sent)
    qkv = [qkv_own, qkv_got, qkv_core, to_core(qkv_got)]
    query, kv = call(
        project_kernel,
        [shape((tokens, 2 * block), HALF), shape((tokens, 4 * block), HALF)],
        [h_one, h_one_far] + qkv + [row_m, row_s],
    )
    kv_far = to_core(kv)
    up_got = to_y(up_own)
    attended, lse = call(
        attend_kernel,
        [shape((tokens, 2 * block), HALF), shape((2 * block // HD, tokens), FLOAT)],
        [query, kv, kv_far],
    )
    attended, o_got, cqo_x, cqo_got = tie(attended, o_got, cqo_x, cqo_got)
    cqo_got_x = to_x(cqo_got)
    outs = [o_own, o_got, o_core, to_core(o_got)]
    attn_near, attn_far = call(out_kernel, [pair_wide, pair_half], [attended] + outs)
    attn_far, ckv_got, text_got = tie(attn_far, ckv_got, text_got)
    attn_far = to_x(attn_far)
    gradient = tokens_sent(cotangent, y)
    down_got = to_y(down_own)

    text_two = cat(
        [
            tail_dot(text_own, ckv_own[:, i * part : (i + 1) * part])
            + tail_dot(text_got, ckv_got[:, i * part : (i + 1) * part])
            for i in range(2)
        ],
        1,
    )
    text_two = half(
        text_two + cat((jnp.zeros((1, block), FLOAT), row_m[:, 3 * block : 4 * block]), 1)
    )
    text_near = cat((text_two, to_core(text_two)), 1)
    cq_bias_row = half(cat((row_m[:, 2 * block : 3 * block], row_s[:, 2 * block : 3 * block]), 1))
    text_far = to_x(cat((text_near, cat((cq_bias_row, cq_bias_row), 1)), 0))
    attn_far, text_far, cqo_got_x = tie(attn_far, text_far, cqo_got_x)
    cqo_all = (
        cqo_own,
        cqo_got,
        to_core(cqo_own),
        to_core(cqo_got),
        cqo_x,
        cqo_got_x,
        to_core(cqo_x),
        to_core(cqo_got_x),
    )
    far_bias = wide(text_far[text_rows:, : 2 * block])
    text_far = text_far[:text_rows]

    attn_out, cross_in, cross_query, cross_att, cross_lse, x_two, h_two = call(
        cross_kernel,
        [
            pair_wide,
            pair_half,
            shape((4, own, block), HALF),
            shape((4, own, block), HALF),
            shape((D // HD, own), FLOAT),
            pair_wide,
            pair_half,
        ],
        [latents, mods, attn_near, attn_far, row_m, row_s, far_bias, text_near, text_far, *cqo_all],
    )

    h_two, up_got, *gradient = tie(h_two, up_got, *gradient)
    h_two_far = to_x(h_two)
    gradient = tokens_got(*gradient, same)
    grad_mlp = half(cat((mods[0, 5:6], mods[1, 5:6]), 1) * wide(gradient))
    h_two_far, grad_mlp = tie(h_two_far, grad_mlp)
    grad_mlp_far = to_x(grad_mlp)
    up = [up_own, up_got, up_core, to_core(up_got)]
    pre, hidden = call(
        up_kernel,
        [shape((2, tokens, ff), FLOAT), shape((2, tokens, ff), HALF)],
        [h_two, h_two_far] + up + [row_m, row_s],
    )
    hidden, grad_mlp_far, down_got = tie(hidden, grad_mlp_far, down_got)

    ff_shape = shape((part, ff), HALF)
    down_keep, down_keep1, down_send, down_send1 = call(
        ff_weight_kernel, [ff_shape] * 4, [grad_mlp, grad_mlp_far, hidden]
    )
    down_keep = half(wide(down_keep) + wide(to_core(down_send)))
    down_far = half(wide(down_keep1) + wide(to_core(down_send1)))
    down_far, down_keep, hidden = tie(down_far, down_keep, hidden)
    down_far = to_y(down_far)
    down = [down_own, down_got, down_core, to_core(down_got)]
    grad_pre, two_near, two_far, pre_sums = call(
        mlp_back_kernel,
        [shape((2, tokens, ff), HALF), pair_wide, pair_half, shape((2, ff), FLOAT)],
        [grad_mlp, grad_mlp_far, pre] + up + down,
    )
    two_far = to_x(two_far)
    up_keep, up_keep1, up_send, up_send1 = call(
        ff_weight_kernel, [ff_shape] * 4, [h_two, h_two_far, grad_pre]
    )
    mlp_near, mlp_far = call(down_kernel, [pair_wide, pair_half], [hidden] + down)
    up_send, up_send1, up_keep, up_keep1, down_far, mlp_far = tie(
        up_send, up_send1, up_keep, up_keep1, down_far, mlp_far
    )
    up_keep = half(wide(up_keep) + wide(to_core(up_send)))
    up_far = half(wide(up_keep1) + wide(to_core(up_send1)))
    two_far, up_far, up_keep = tie(two_far, up_far, up_keep)
    up_far = to_y(up_far)
    down_sum = DpSum(half(wide(down_keep) + wide(down_far)))
    down_sum.send()

    text_shape = shape((text_rows, 4 * block), HALF)
    grad_cross, grad_cq, text_grad_near, text_grad_far, grad_x_one, grad_attn, cross_sums = call(
        cross_back_kernel,
        [
            pair_half,
            shape((4, own, block), HALF),
            text_shape,
            text_shape,
            pair_wide,
            pair_half,
            shape((2, 5, part), FLOAT),
        ],
        [gradient, mods, x_two, two_near, two_far, attn_out, cross_query, cross_lse, text_near, text_far, *cqo_all],
        [pltpu.VMEM((own, block), HALF)],
    )
    (grad_attn,) = tie_sums([down_sum], grad_attn)
    grad_attn_far = to_x(grad_attn)
    down_sum.send()
    cqo_shape = shape((block, 2 * D), HALF)
    cqo_keep, cqo_keep_x, cqo_send, cqo_send_x = call(
        cross_weight_kernel, [cqo_shape] * 4, [cross_in, grad_cross, grad_cq, cross_att]
    )
    text_grad_core = to_core(cat((text_grad_near[:, 2 * block :], text_grad_far[:, 2 * block :]), 1))
    cqo_keep = half(wide(cqo_keep) + wide(to_core(cqo_send)))
    cqo_far = half(wide(cqo_keep_x) + wide(to_core(cqo_send_x)))
    text_chip = half(
        wide(cat((text_grad_near[:, : 2 * block], text_grad_far[:, : 2 * block]), 1))
        + wide(text_grad_core)
    )
    grad_attn_far, up_far, cqo_far, text_chip, mlp_far = tie_sums(
        [down_sum], grad_attn_far, up_far, cqo_far, text_chip, mlp_far
    )

    up_sum = DpSum(half(wide(up_keep) + wide(up_far)))
    up_sum.send()
    down_sum.send()
    cqo_far = to_x(cqo_far)
    text_from = to_x(text_chip[:, 2 * block :])
    o_shape = shape((block, D), HALF)
    grad_att, o_keep, o_send = call(
        out_back_kernel,
        [shape((tokens, 2 * block), HALF), o_shape, o_shape],
        [grad_attn, grad_attn_far, attended] + outs,
    )
    grad_att, cqo_far, text_from = tie(grad_att, cqo_far, text_from)
    rest_shape = shape((block, 5 * part), HALF)
    rest_keep, rest_far, grad_text, text_part, cv_sum = call(
        rest_kernel,
        [
            rest_shape,
            rest_shape,
            shape((text_rows, 2 * block), HALF),
            shape((text_rows, D), HALF),
            shape((1, block), FLOAT),
        ],
        [
            cqo_keep,
            cqo_far,
            text_chip[:, : 2 * block],
            text_from,
            text_own,
            text_got,
            ckv_own,
            ckv_got,
            o_keep,
            to_core(o_send),
        ],
    )
    rest_far, mlp_far, grad_att = tie(rest_far, mlp_far, grad_att)
    rest_far = to_y(rest_far)
    mlp_far = to_x(mlp_far)
    grad_query, kv_keep, kv_send = call(
        attend_back_kernel,
        [
            shape((tokens, 2 * block), HALF),
            shape((tokens, 4 * block), FLOAT),
            shape((tokens, 4 * block), HALF),
        ],
        [query, kv, kv_far, lse, grad_att],
    )
    grad_query, kv_keep, kv_send, mlp_far = tie_sums(
        [up_sum, down_sum], grad_query, kv_keep, kv_send, mlp_far
    )
    up_sum.send()
    down_sum.send()
    kv_got = to_core(kv_send)
    layer_pair, layer_sums = call(
        layer_out_kernel,
        [pair_half, shape((2, 2, part), FLOAT)],
        [mlp_near, mlp_far, x_two, mods, gradient, grad_mlp],
    )
    layer_pair = halves_sent(layer_pair, same)
    text_near = to_core(text_part)
    grad_shape = shape((tokens, 3 * block), HALF)
    near, far, grad_m, grad_s, qkv_sums = call(
        project_back_kernel,
        [pair_wide, pair_half, grad_shape, grad_shape, shape((2, 3 * block), FLOAT)],
        [grad_query, kv_keep, kv_got] + qkv,
    )
    far, text_near, rest_far, *layer_pair = tie(far, text_near, rest_far, *layer_pair)
    far = to_x(far)
    rest_sum = DpSum(half(wide(rest_keep) + wide(rest_far)))
    rest_sum.send()
    layer_out = halves_got(*layer_pair, y)
    text_sum = wide(text_part) + wide(text_near)
    text_got = to_x(half(text_sum))
    qkv_shape = shape((block, 3 * part), HALF)
    qkv_keep, qkv_keep1, qkv_send, qkv_send1 = call(
        project_weight_kernel, [qkv_shape] * 4, [h_one, h_one_far, grad_m, grad_s]
    )
    qkv_send, qkv_send1, qkv_keep, qkv_keep1, text_got = tie_sums(
        [up_sum, down_sum], qkv_send, qkv_send1, qkv_keep, qkv_keep1, text_got
    )
    up_sum.send()
    qkv_far = to_y(half(wide(qkv_keep1) + wide(to_core(qkv_send1))))
    qkv_keep = half(wide(qkv_keep) + wide(to_core(qkv_send)))
    text_sum = text_sum + wide(text_got)
    text_far = to_y(half(text_sum[:, part:]))
    far, text_far = tie_sums([rest_sum], far, text_far)
    rest_sum.send()
    text_grad = in_order(text_sum[:, :part], wide(text_far))
    token_pair, one_sums = call(
        norm_back_kernel,
        [pair_half, shape((2, 2, part), FLOAT)],
        [latents, mods, near, far, grad_x_one],
    )
    token_sent = halves_sent(token_pair, same)
    (qkv_far,) = tie_sums([rest_sum, up_sum], qkv_far)
    qkv_sum = DpSum(half(wide(qkv_keep) + wide(qkv_far)))
    qkv_sum.send()
    rest_sum.send()
    up_sum.send()
    token_input_gradient = wide(halves_got(*token_sent, y))

    feature_sums = cat((one_sums, cross_sums, layer_sums), 1)
    flat = feature_sums.reshape(9 * D)
    gcq_sum = jnp.sum(wide(grad_cq), 1)
    cv_sum = cv_sum[0]
    core_got = to_core(
        cat((flat, gcq_sum[3], gcq_sum[1], qkv_sums[1, :block], qkv_sums[1, 2 * block :], pre_sums[1]), 0)
    )
    chip = core_got + cat(
        (flat, gcq_sum[2], gcq_sum[0], qkv_sums[0, :block], qkv_sums[0, 2 * block :], pre_sums[0]), 0
    )
    x_got = to_x(chip[: 9 * D + block])
    sums = (chip[: 9 * D] + x_got[: 9 * D]).reshape(2, 9, part)
    cq_row = chip[9 * D + block : 9 * D + 2 * block] + x_got[9 * D :]
    rest = chip[9 * D + 2 * block :]
    row_rows = [
        (v[: v.shape[0] // 2], v[v.shape[0] // 2 :])
        for v in (rest[:block], rest[block : 2 * block], cq_row, cv_sum, rest[2 * block :])
    ]
    row_low = cat([v[0] for v in row_rows], 0)
    row_high = cat([v[1] for v in row_rows], 0)
    row_mine = jnp.where(first_col, row_low, row_high)
    row_sent = jnp.where(first_col, row_high, row_low)
    col_got = to_y(cat((sums[1].reshape(9 * part), row_sent), 0))
    sums_got = col_got[: 9 * part].reshape(9, part)
    sums_own = sums[0]

    def six(v):
        return jnp.stack((v[0], v[1], v[5], v[2], v[3], v[7]))

    time_own, time_got = six(sums_own), six(sums_got)
    time_grad = jnp.where(first_col, jnp.stack((time_own, time_got)), jnp.stack((time_got, time_own)))
    totals = small_sum_over_dp(
        cat(((sums_own + sums_got).reshape(9 * part), row_mine + col_got[9 * part :]), 0)
    )
    table_grad = six(totals[: 9 * part].reshape(9, part))
    o_bias_grad, co_bias_grad, down_bias_grad = (
        totals[i * part : (i + 1) * part] for i in (6, 4, 8)
    )
    rows = totals[9 * part :]
    q_bias_grad, v_bias_grad, cq_bias_grad, cv_bias_grad = (
        rows[i * quarter : (i + 1) * quarter] for i in range(4)
    )
    up_bias_grad = rows[4 * quarter :]

    qkv_grad, rest_sum = qkv_sum.finish(), rest_sum.finish()
    up_sum, down_sum = up_sum.finish(), down_sum.finish()
    q_grad, k_grad, v_grad = (wide(qkv_grad[:, i * part : (i + 1) * part]).T for i in range(3))
    cq_grad, co_grad, ck_grad, cv_grad, o_grad = (
        wide(rest_sum[:, i * part : (i + 1) * part]) for i in range(5)
    )
    return (
        layer_out,
        token_input_gradient,
        text_grad,
        time_grad,
        table_grad,
        q_grad,
        k_grad,
        v_grad,
        q_bias_grad,
        v_bias_grad,
        o_grad,
        o_bias_grad,
        cq_grad.T,
        cq_bias_grad,
        ck_grad.T,
        cv_grad.T,
        cv_bias_grad,
        co_grad,
        co_bias_grad,
        wide(up_sum),
        up_bias_grad,
        wide(down_sum).T,
        down_bias_grad,
    )


def solution(mesh):
    in_specs = (
        P(("dp", "row"), "col"),
        P("dp", "col"),
        P("dp", None, "col"),
        P(None, "col"),
        P("col", "row"),
        P("col", "row"),
        P("col", "row"),
        P(("row", "col")),
        P(("row", "col")),
        P("row", "col"),
        P("col"),
        P("col", "row"),
        P(("row", "col")),
        P("col", "row"),
        P("col", "row"),
        P(("row", "col")),
        P("row", "col"),
        P("col"),
        P("col", "row"),
        P(("row", "col")),
        P("row", "col"),
        P("col"),
        P(("dp", "row"), "col"),
    )
    out_specs = (
        P(("dp", "row"), "col"),
        P(("dp", "row"), "col"),
        P("dp", "col"),
        P("dp", None, "col"),
        P(None, "col"),
        P("col", "row"),
        P("col", "row"),
        P("col", "row"),
        P(("row", "col")),
        P(("row", "col")),
        P("row", "col"),
        P("col"),
        P("col", "row"),
        P(("row", "col")),
        P("col", "row"),
        P("col", "row"),
        P(("row", "col")),
        P("row", "col"),
        P("col"),
        P("col", "row"),
        P(("row", "col")),
        P("row", "col"),
        P("col"),
    )
    return jax.shard_map(
        on_device, mesh=mesh, in_specs=in_specs, out_specs=out_specs, check_vma=False
    )
```

time: 1560 us -> 603 us (0.39)
  waiting for transfers between devices: 1170 us -> 240 us
  matrix products: 160 us -> 4.51 us
  Pallas kernels: 0 us -> 152 us
  starting transfers between devices: 2.76 us -> 88 us
  blocking collectives: 60.7 us -> 0 us
  other arithmetic: 89.8 us -> 51.8 us
    reduce_scatter x16 -> x0, waiting for transfers between devices: 605 us -> none  [the longest x6 271 us: rows_out(): lax.psum_scatter(terms(jnp.int32(0), tok_rows * lax.axis_size('row')), 'r...]
    all_gather x14 -> x0, waiting for transfers between devices: 339 us -> none  [the longest x6 133 us: rows_in(): return lax.all_gather(value, 'row', axis=0, tiled=True)]
    ppermute x0 -> x84, waiting for transfers between devices: none -> 240 us  [the longest x15 81.6 us: to_x(): return lax.ppermute(value, 'row', ACROSS)]
    psum x2 -> x0, waiting for transfers between devices: 227 us -> none  [the longest x1 207 us: on_device(): lax.psum(q_weight_grad.astype(jnp.bfloat16), 'dp').astype(jnp.float32)]
    pallas_call x0 -> x20, Pallas kernels: none -> 152 us  [call(): pl.pallas_call(kernel, out_shape=outs, in_specs=specs, out_specs=[vmem] *...]
    dot_general x50 -> x0, matrix products: 122 us -> none  [the longest x10 45.8 us: plain_dot(): return jnp.dot(left, right, preferred_element_type=FLOAT)]
    ppermute x0 -> x84, starting transfers between devices: none -> 88 us  [the longest x15 20.7 us: to_x(): return lax.ppermute(value, 'row', ACROSS)]
    psum x6 -> x0, blocking collectives: 50.7 us -> none  [the longest x4 21.3 us: col_sums(): return lax.psum((first, second), 'col')]
  transfers between devices with their start and end apart: 32 -> 84, of which waited for: 31 -> 27; matrix products, arithmetic and copies ran while one was open for 9% -> 13% of each run, Pallas kernels for 0% -> 23%
where the time goes in v1:
time: 603 us; the launch traced here: 591 us
  waiting for transfers between devices  240 us (40%)
  Pallas kernels  152 us (25%)
  starting transfers between devices  88 us (15%)
  local copies, waits for them, and re-layouts  52.1 us (9%)
  other arithmetic  51.8 us (9%)
    pallas_call x20, Pallas kernels, call(): pl.pallas_call(kernel, out_shape=outs, in_specs=specs, out_specs=[vmem] *...  152 us
    ppermute x15, waiting for transfers between devices, to_x(): return lax.ppermute(value, 'row', ACROSS)  81.6 us
    ppermute x8, waiting for transfers between devices, gather_sent(): return (value, lax.ppermute(value, 'dp', dp_pairs(step)))  79.2 us
    unnamed x264, local copies, waits for them, and re-layouts  35.6 us
    ppermute x14, waiting for transfers between devices, to_y(): return lax.ppermute(value, 'col', SWAP)  32.6 us
    ppermute x8, waiting for transfers between devices, reduce_sent(): got = lax.ppermute(jnp.where(upper, low, high), 'dp', dp_pairs(step))  28.3 us
    convert_element_type x23, other arithmetic, half(): return value.astype(HALF)  23.1 us
    ppermute x15, starting transfers between devices, to_x(): return lax.ppermute(value, 'row', ACROSS)  20.7 us
  transfers between devices with their start and end apart: 84, of which 27 were waited for; matrix products, arithmetic and copies ran while one was open for 13% of the time, Pallas kernels for 23%

profile of v1, /device:TPU:0, one launch (start us, length us, event | category | flops | bytes accessed | tf_op | source)
XLA Modules:
  0.0 591.5 jit_solution(10961757263554014886)
XLA Ops:
  3.2 3.9 collective-permute-start
  7.1 2.5 collective-permute-start.1
  11.6 2.2 concatenate.140.own_m
  13.9 4.3 collective-permute-done.2
  21.8 2.6 collective-permute-start.3
  24.4 12.5 %collective-permute-done.3.far = bf16[256,1152]{1,0:T(8,128)(2,1)S(1)} collective-permute-done((bf16[256,1152]{1,0:T(8,128)(2,1)S(1)}, bf16[256,1152]{1,0:T(8,128)(2,1)S(1)}, u32[]{:S(2)}, u32[]{:S(2)}) %collective-permute-start.3) | collective-permute-done | bytes 589856 | tf_op jit(solution)/shard_map/ppermute | solution.py:37
  37.7 5.0 collective-permute-done.4.got_m
  46.8 7.9 %shard_map.400 = (bf16[512,576]{1,0:T(8,128)(2,1)S(1)}, bf16[512,1152]{1,0:T(8,128)(2,1)}) custom-call(bf16[256,1152]{1,0:T(8,128)(2,1)S(1)} %shard_map.398.near, bf16[256,1152]{1,0:T(8,128)(2,1)S(1)} %copy-done.31, bf16[288,1728]{1,0:T(8,128)(2,1)S(1)} %concatenate.140.own_m, bf16[288,1728]{1,0:T(8,128)(2,1)} %collective-permute-done.4.got_m, ...), custom_call_target="tpu_custom_call" | custom-call | flops 1 | bytes 1 | tf_op jit(solution)/shard_map/pallas_call | solution.py:129
  66.5 12.9 %shard_map.401 = (bf16[512,576]{1,0:T(8,128)(2,1)S(1)}, f32[8,512]{1,0:T(8,128)S(1)}) custom-call(bf16[512,576]{1,0:T(8,128)(2,1)S(1)} %copy-done.24, bf16[512,1152]{1,0:T(8,128)(2,1)S(1)} %copy-done.12, bf16[512,1152]{1,0:T(8,128)(2,1)} %collective-permute-done.8.far), custom_call_target="tpu_custom_call" | custom-call | flops 1 | bytes 1 | tf_op jit(solution)/shard_map/pallas_call | solution.py:129
  79.5 1.8 collective-permute-done.9.got_m
  81.4 1.8 collective-permute-start.15
  85.0 3.0 shard_map.402
  88.9 9.3 %collective-permute-done.15.text_other = bf16[120,576]{1,0:T(8,128)(2,1)S(1)} collective-permute-done((bf16[120,576]{1,0:T(8,128)(2,1)S(1)}, bf16[120,576]{1,0:T(8,128)(2,1)S(1)}, u32[]{:S(2)}, u32[]{:S(2)}) %collective-permute-start.15) | collective-permute-done | bytes 138272 | tf_op jit(solution)/shard_map/ppermute | solution.py:41
  105.1 1.8 collective-permute-start.24
  113.9 1.9 copy.92
  117.1 13.4 %collective-permute-done.18 = bf16[121,1152]{1,0:T(8,128)(2,1)} collective-permute-done((bf16[121,1152]{1,0:T(8,128)(2,1)}, bf16[121,1152]{1,0:T(8,128)(2,1)}, u32[]{:S(2)}, u32[]{:S(2)}) %collective-permute-start.18) | collective-permute-done | bytes 278816 | tf_op jit(solution)/shard_map/ppermute | solution.py:37
  132.4 3.6 collective-permute-start.26
  139.8 14.3 %shard_map.403 = (f32[256,1152]{1,0:T(8,128)}, bf16[256,1152]{1,0:T(8,128)(2,1)S(1)}, bf16[4,256,288]{2,1,0:T(8,128)(2,1)}, bf16[4,256,288]{2,1,0:T(8,128)(2,1)}...) custom-call(bf16[256,1152]{1,0:T(8,128)(2,1)S(1)} %pad_maximum_fusion.6.x_ref, ...), custom_call_target="tpu_custom_call" | custom-call | flops 1 | bytes 1 | tf_op jit(solution)/shard_map/pallas_call | solution.py:129
  154.8 2.1 collective-permute-start.27
  157.9 12.5 %collective-permute-done.27.far = bf16[256,1152]{1,0:T(8,128)(2,1)S(1)} collective-permute-done((bf16[256,1152]{1,0:T(8,128)(2,1)S(1)}, bf16[256,1152]{1,0:T(8,128)(2,1)S(1)}, u32[]{:S(2)}, u32[]{:S(2)}) %collective-permute-start.27) | collective-permute-done | bytes 589856 | tf_op jit(solution)/shard_map/ppermute | solution.py:37
  173.3 9.3 %shard_map.404 = (f32[2,512,1152]{2,1,0:T(8,128)}, bf16[2,512,1152]{2,1,0:T(8,128)(2,1)}) custom-call(bf16[256,1152]{1,0:T(8,128)(2,1)S(1)} %get-tuple-element.203.near, bf16[256,1152]{1,0:T(8,128)(2,1)S(1)} %collective-permute-done.27.far, bf16[576,1152]{1,0:T(8,128)(2,1)S(1)} %copy-done.3, bf16[576,1152]{1,0:T(8,128)(2,1)} %collective-permute-done.24.got_m.refs_1_, ...), custom_call_target="tpu_custom_call" | custom-call | flops 1 | bytes 1 | tf_op jit(solution)/shard_map/pallas_call | solution.py:129
  182.7 2.7 collective-permute-done.30.g_far.far
  185.3 6.1 %shard_map.407 = (bf16[576,1152]{1,0:T(8,128)(2,1)S(1)}, bf16[576,1152]{1,0:T(8,128)(2,1)S(1)}, bf16[576,1152]{1,0:T(8,128)(2,1)S(1)}, bf16[576,1152]{1,0:T(8,128)(2,1)}) custom-call(bf16[256,1152]{1,0:T(8,128)(2,1)S(1)} %get-tuple-element.204.g_near.near.gm_ref, bf16[256,1152]{1,0:T(8,128)(2,1)S(1)} %collective-permute-done.30.g_far.far, ...), custom_call_target="tpu_custom_call" | custom-call | flops 1 | bytes 1 | tf_op jit(solution)/shard_map/pallas_call | solution.py:129
  192.5 4.1 collective-permute-done.35
  202.1 15.0 %shard_map.405 = (bf16[2,512,1152]{2,1,0:T(8,128)(2,1)}, f32[256,1152]{1,0:T(8,128)S(1)}, bf16[256,1152]{1,0:T(8,128)(2,1)S(1)}, f32[2,1152]{1,0:T(2,128)S(1)}) custom-call(bf16[256,1152]{1,0:T(8,128)(2,1)S(1)} %get-tuple-element.204.g_near.near.gm_ref, bf16[256,1152]{1,0:T(8,128)(2,1)S(1)} %collective-permute-done.30.g_far.far, ...), custom_call_target="tpu_custom_call" | custom-call | flops 1 | bytes 1 | tf_op jit(solution)/shard_map/pallas_call | solution.py:129
  219.0 6.2 %shard_map.406 = (bf16[576,1152]{1,0:T(8,128)(2,1)S(1)}, bf16[576,1152]{1,0:T(8,128)(2,1)S(1)}, bf16[576,1152]{1,0:T(8,128)(2,1)S(1)}, bf16[576,1152]{1,0:T(8,128)(2,1)}) custom-call(bf16[256,1152]{1,0:T(8,128)(2,1)S(1)} %get-tuple-element.203.near, bf16[256,1152]{1,0:T(8,128)(2,1)S(1)} %collective-permute-done.27.far, ...), custom_call_target="tpu_custom_call" | custom-call | flops 1 | bytes 1 | tf_op jit(solution)/shard_map/pallas_call | solution.py:129
  228.6 6.9 %shard_map.408 = (f32[256,1152]{1,0:T(8,128)S(1)}, bf16[256,1152]{1,0:T(8,128)(2,1)S(1)}) custom-call(bf16[2,512,1152]{2,1,0:T(8,128)(2,1)} %get-tuple-element.224.ff.hidden, bf16[576,1152]{1,0:T(8,128)(2,1)S(1)} %bitcast.45, bf16[576,1152]{1,0:T(8,128)(2,1)S(1)} %copy-done.8, bf16[576,1152]{1,0:T(8,128)(2,1)S(1)} %copy-done.10, bf16[576,1152]{1,0:T(8,128)(2,1)} %copy-done.75), custom_call_target="tpu_custom_call" | custom-call | flops 1 | bytes 1 | tf_op jit(solution)/shard_map/pallas_call | solution.py:129
  240.8 2.0 add_convert_fusion.3
  247.4 7.0 %collective-permute-done.34.far = bf16[256,1152]{1,0:T(8,128)(2,1)S(1)} collective-permute-done((bf16[256,1152]{1,0:T(8,128)(2,1)}, bf16[256,1152]{1,0:T(8,128)(2,1)S(1)}, u32[]{:S(2)}, u32[]{:S(2)}) %collective-permute-start.34) | collective-permute-done | bytes 589856 | tf_op jit(solution)/shard_map/ppermute | solution.py:37
  254.5 18.2 %shard_map.409 = (bf16[256,1152]{1,0:T(8,128)(2,1)S(1)}, bf16[4,256,288]{2,1,0:T(8,128)(2,1)}, bf16[120,1152]{1,0:T(8,128)(2,1)S(1)}, bf16[120,1152]{1,0:T(8,128...) custom-call(bf16[256,1152]{1,0:T(8,128)(2,1)S(1)} %copy-done.2, ...), custom_call_target="tpu_custom_call" | custom-call | flops 1 | bytes 1 | tf_op jit(solution)/shard_map/pallas_call | solution.py:129
  273.8 4.9 shard_map.410
  282.3 2.3 collective-permute-done.45
  284.6 2.6 collective-permute-start.46
  288.9 13.5 %collective-permute-done.46 = bf16[144,1152]{1,0:T(8,128)(2,1)S(1)} collective-permute-done((bf16[144,1152]{1,0:T(8,128)(2,1)S(1)}, bf16[144,1152]{1,0:T(8,128)(2,1)S(1)}, u32[]{:S(2)}, u32[]{:S(2)}) %collective-permute-start.46) | collective-permute-done | bytes 331808 | tf_op jit(solution)/shard_map/ppermute | solution.py:538
  302.5 9.2 %collective-permute-done.43 = bf16[576,1152]{1,0:T(8,128)(2,1)S(1)} collective-permute-done((bf16[576,1152]{1,0:T(8,128)(2,1)S(1)}, bf16[576,1152]{1,0:T(8,128)(2,1)S(1)}, u32[]{:S(2)}, u32[]{:S(2)}) %collective-permute-start.43) | collective-permute-done | bytes 1327136 | tf_op jit(solution)/shard_map/ppermute | solution.py:41
  313.9 3.8 shard_map.411
  322.4 23.3 %collective-permute-done.48.text_got = bf16[120,576]{1,0:T(8,128)(2,1)S(1)} collective-permute-done((bf16[120,576]{1,0:T(8,128)(2,1)S(1)}, bf16[120,576]{1,0:T(8,128)(2,1)S(1)}, u32[]{:S(2)}, u32[]{:S(2)}) %collective-permute-start.48) | collective-permute-done | bytes 138272 | tf_op jit(solution)/shard_map/ppermute | solution.py:37
  345.7 4.9 shard_map.412
  351.3 2.5 collective-permute-start.52
  355.3 20.2 %shard_map.413 = (bf16[512,576]{1,0:T(8,128)(2,1)S(1)}, f32[512,1152]{1,0:T(8,128)}, bf16[512,1152]{1,0:T(8,128)(2,1)S(1)}) custom-call(bf16[512,576]{1,0:T(8,128)(2,1)S(1)} %copy-done.25, bf16[512,1152]{1,0:T(8,128)(2,1)S(1)} %copy-done.13, bf16[512,1152]{1,0:T(8,128)(2,1)} %collective-permute-done.8.far, f32[8,512]{1,0:T(8,128)S(1)} %copy-done.66, ...), custom_call_target="tpu_custom_call" | custom-call | flops 1 | bytes 1 | tf_op jit(solution)/shard_map/pallas_call | solution.py:129
  378.8 4.2 collective-permute-start.57
  386.1 7.7 %shard_map.414 = (f32[256,1152]{1,0:T(8,128)}, bf16[256,1152]{1,0:T(8,128)(2,1)S(1)}, bf16[512,864]{1,0:T(8,128)(2,1)S(1)}, bf16[512,864]{1,0:T(8,128)(2,1)S(1)}, f32[2,864]{1,0:T(2,128)S(1)}) custom-call(bf16[512,576]{1,0:T(8,128)(2,1)S(1)} %get-tuple-element.271.gq, f32[512,1152]{1,0:T(8,128)} %get-tuple-element.272.keep, bf16[512,1152]{1,0:T(8,128)(2,1)} %copy-done.87, ...), custom_call_target="tpu_custom_call" | custom-call | flops 1 | bytes 1 | tf_op jit(solution)/shard_map/pallas_call | solution.py:129
  397.3 9.2 %collective-permute-done.57 = bf16[256,576]{1,0:T(8,128)(2,1)S(1)} collective-permute-done((bf16[256,576]{1,0:T(8,128)(2,1)S(1)}, bf16[256,576]{1,0:T(8,128)(2,1)S(1)}, u32[]{:S(2)}, u32[]{:S(2)}) %collective-permute-start.57) | collective-permute-done | bytes 294944 | tf_op jit(solution)/shard_map/ppermute | solution.py:87
  408.8 3.2 collective-permute-start.58
  412.2 2.4 add_convert_fusion
  417.3 6.8 %shard_map.416 = (bf16[288,1728]{1,0:T(8,128)(2,1)S(1)}, bf16[288,1728]{1,0:T(8,128)(2,1)S(1)}, bf16[288,1728]{1,0:T(8,128)(2,1)}, bf16[288,1728]{1,0:T(8,128)(2,1)}) custom-call(bf16[256,1152]{1,0:T(8,128)(2,1)S(1)} %copy-done.1, bf16[256,1152]{1,0:T(8,128)(2,1)S(1)} %copy-done.32, bf16[512,864]{1,0:T(8,128)(2,1)S(1)} %copy-done.54, ...), custom_call_target="tpu_custom_call" | custom-call | flops 1 | bytes 1 | tf_op jit(solution)/shard_map/pallas_call | solution.py:129
  424.8 6.5 %collective-permute-done.59 = bf16[120,1152]{1,0:T(8,128)(2,1)S(1)} collective-permute-done((bf16[120,1152]{1,0:T(8,128)(2,1)S(1)}, bf16[120,1152]{1,0:T(8,128)(2,1)S(1)}, u32[]{:S(2)}, u32[]{:S(2)}) %collective-permute-start.59) | collective-permute-done | bytes 276512 | tf_op jit(solution)/shard_map/ppermute | solution.py:37
  434.6 1.8 add_convert_fusion.17
  436.4 1.9 convert_bitcast_fusion
  441.5 3.9 collective-permute-start.64
  451.0 3.7 collective-permute-done.67
  456.1 3.0 collective-permute-done.68
  461.7 2.8 collective-permute-start.70
  464.4 2.4 add_convert_fusion.10
  471.6 2.7 collective-permute-start.76
  478.3 23.2 %collective-permute-done.76 = bf16[144,1152]{1,0:T(8,128)(2,1)} collective-permute-done((bf16[144,1152]{1,0:T(8,128)(2,1)S(1)}, bf16[144,1152]{1,0:T(8,128)(2,1)}, u32[]{:S(2)}, u32[]{:S(2)}) %collective-permute-start.76) | collective-permute-done | bytes 331808 | tf_op jit(solution)/shard_map/ppermute | solution.py:547
  501.6 1.9 add_convert_fusion.9
  508.7 18.7 %collective-permute-done.81 = bf16[72,2880]{1,0:T(8,128)(2,1)S(1)} collective-permute-done((bf16[72,2880]{1,0:T(8,128)(2,1)S(1)}, bf16[72,2880]{1,0:T(8,128)(2,1)S(1)}, u32[]{:S(2)}, u32[]{:S(2)}) %collective-permute-start.81) | collective-permute-done | bytes 414752 | tf_op jit(solution)/shard_map/ppermute | solution.py:547
  529.3 17.8 %collective-permute-done.83 = bf16[288,1152]{1,0:T(8,128)(2,1)S(1)} collective-permute-done((bf16[288,1152]{1,0:T(8,128)(2,1)S(1)}, bf16[288,1152]{1,0:T(8,128)(2,1)S(1)}, u32[]{:S(2)}, u32[]{:S(2)}) %collective-permute-start.83) | collective-permute-done | bytes 663584 | tf_op jit(solution)/shard_map/ppermute | solution.py:547
  547.3 14.7 %collective-permute-done.78 = bf16[72,1728]{1,0:T(8,128)(2,1)S(1)} collective-permute-done((bf16[72,1728]{1,0:T(8,128)(2,1)S(1)}, bf16[72,1728]{1,0:T(8,128)(2,1)S(1)}, u32[]{:S(2)}, u32[]{:S(2)}) %collective-permute-start.78) | collective-permute-done | bytes 248864 | tf_op jit(solution)/shard_map/ppermute | solution.py:538
  562.2 3.4 collective-permute-start.79
  567.3 9.6 %collective-permute-done.79 = bf16[72,1728]{1,0:T(8,128)(2,1)S(1)} collective-permute-done((bf16[72,1728]{1,0:T(8,128)(2,1)S(1)}, bf16[72,1728]{1,0:T(8,128)(2,1)S(1)}, u32[]{:S(2)}, u32[]{:S(2)}) %collective-permute-start.79) | collective-permute-done | bytes 248864 | tf_op jit(solution)/shard_map/ppermute | solution.py:547
  577.4 2.2 fusion.8
  579.6 9.9 %collective-permute-done.80 = bf16[144,1728]{1,0:T(8,128)(2,1)S(1)} collective-permute-done((bf16[144,1728]{1,0:T(8,128)(2,1)S(1)}, bf16[144,1728]{1,0:T(8,128)(2,1)S(1)}, u32[]{:S(2)}, u32[]{:S(2)}) %collective-permute-start.80) | collective-permute-done | bytes 497696 | tf_op jit(solution)/shard_map/ppermute | solution.py:547
  (549 shorter events, 140.6 us)
Async XLA Ops:
  3.2 16.3 %collective-permute-start = (bf16[256,576]{1,0:T(8,128)(2,1)}, bf16[256,576]{1,0:T(8,128)(2,1)}, u32[]{:S(2)}, u32[]{:S(2)}) collective-permute-start(bf16[256,576]{1,0:T(8,128)(2,1)} %get-tuple-element.448), channel_id=1, source_target_pairs={{0,0},{1,4},{2,2},{3,6},{4,1},{5,5},{6,3},{7,7},{8,8},{9,12},{10,1... | collective-permute-start | bytes 884744 | tf_op jit(solution)/shard_map/ppermute | solution.py:75
  7.1 12.5 %collective-permute-start.1 = (bf16[256,576]{1,0:T(8,128)(2,1)}, bf16[256,576]{1,0:T(8,128)(2,1)}, u32[]{:S(2)}, u32[]{:S(2)}) collective-permute-start(bf16[256,576]{1,0:T(8,128)(2,1)} %get-tuple-element.449), channel_id=1, source_target_pairs={{0,4},{1,0},{2,6},{3,2},{4,5},{5,1},{6,7},{7,3},{8,12},{9,8},{10,1... | collective-permute-start | bytes 884744 | tf_op jit(solution)/shard_map/ppermute | solution.py:76
  18.2 24.5 %collective-permute-start.4 = (bf16[288,1728]{1,0:T(8,128)(2,1)S(1)}, bf16[288,1728]{1,0:T(8,128)(2,1)}, u32[]{:S(2)}, u32[]{:S(2)}) collective-permute-start(bf16[288,1728]{1,0:T(8,128)(2,1)S(1)} %concatenate.140.own_m), channel_id=1, source_target_pairs={{0,1},{1,0},{2,3},{3,2},{4,5},{5,4},{6,7},{7,6},{8,9},{9,8},{10,11... | collective-permute-start | bytes 2985992 | tf_op jit(solution)/shard_map/ppermute | solution.py:41
  21.8 15.1 %collective-permute-start.3 = (bf16[256,1152]{1,0:T(8,128)(2,1)S(1)}, bf16[256,1152]{1,0:T(8,128)(2,1)S(1)}, u32[]{:S(2)}, u32[]{:S(2)}) collective-permute-start(bf16[256,1152]{1,0:T(8,128)(2,1)S(1)} %shard_map.398.near), channel_id=1, source_target_pairs={{0,4},{2,6},{4,0},{6,2},{1,5},{3,7},{5,1},{7,3},{8,12},{10,14},{12... | collective-permute-start | bytes 1769480 | tf_op jit(solution)/shard_map/ppermute | solution.py:37
  24.4 21.0 %collective-permute-start.5 = (bf16[288,1728]{1,0:T(8,128)(2,1)S(1)}, bf16[288,1728]{1,0:T(8,128)(2,1)}, u32[]{:S(2)}, u32[]{:S(2)}) collective-permute-start(bf16[288,1728]{1,0:T(8,128)(2,1)S(1)} %concatenate.140.own_m), channel_id=1, source_target_pairs={{0,2},{2,0},{4,6},{6,4},{1,3},{3,1},{5,7},{7,5},{8,10},{10,8},{12,... | collective-permute-start | bytes 2985992 | tf_op jit(solution)/shard_map/ppermute | solution.py:33
  55.5 8.7 %collective-permute-start.8 = (bf16[512,1152]{1,0:T(8,128)(2,1)}, bf16[512,1152]{1,0:T(8,128)(2,1)}, u32[]{:S(2)}, u32[]{:S(2)}) collective-permute-start(bf16[512,1152]{1,0:T(8,128)(2,1)} %get-tuple-element.181.near), channel_id=1, source_target_pairs={{0,2},{2,0},{4,6},{6,4},{1,3},{3,1},{5,7},{7,5},{8,10},{10,8},{12,... | collective-permute-start | bytes 3538952 | tf_op jit(solution)/shard_map/ppermute | solution.py:33
  55.6 25.6 %collective-permute-start.11 = (bf16[288,1152]{1,0:T(8,128)(2,1)S(1)}, bf16[288,1152]{1,0:T(8,128)(2,1)}, u32[]{:S(2)}, u32[]{:S(2)}) collective-permute-start(bf16[288,1152]{1,0:T(8,128)(2,1)S(1)} %get-tuple-element.184.refs_0_), channel_id=1, source_target_pairs={{0,1},{1,0},{2,3},{3,2},{4,5},{5,4},{6,7},{7,6},{8,9},{9,8},{10,11... | collective-permute-start | bytes 1990664 | tf_op jit(solution)/shard_map/ppermute | solution.py:41
  57.4 23.9 %collective-permute-start.10 = (bf16[288,1152]{1,0:T(8,128)(2,1)S(1)}, bf16[288,1152]{1,0:T(8,128)(2,1)}, u32[]{:S(2)}, u32[]{:S(2)}) collective-permute-start(bf16[288,1152]{1,0:T(8,128)(2,1)S(1)} %get-tuple-element.184.refs_0_), channel_id=1, source_target_pairs={{0,4},{2,6},{4,0},{6,2},{1,5},{3,7},{5,1},{7,3},{8,12},{10,14},{12... | collective-permute-start | bytes 1990664 | tf_op jit(solution)/shard_map/ppermute | solution.py:37
  58.9 22.4 %collective-permute-start.9 = (bf16[288,576]{1,0:T(8,128)(2,1)}, bf16[288,576]{1,0:T(8,128)(2,1)S(1)}, u32[]{:S(2)}, u32[]{:S(2)}) collective-permute-start(bf16[288,576]{1,0:T(8,128)(2,1)} %own_m.5), channel_id=1, source_target_pairs={{0,1},{1,0},{2,3},{3,2},{4,5},{5,4},{6,7},{7,6},{8,9},{9,8},{10,11... | collective-permute-start | bytes 995336 | tf_op jit(solution)/shard_map/ppermute | solution.py:41
  59.3 38.9 %collective-permute-start.14 = (bf16[288,1152]{1,0:T(8,128)(2,1)S(1)}, bf16[288,1152]{1,0:T(8,128)(2,1)}, u32[]{:S(2)}, u32[]{:S(2)}) collective-permute-start(bf16[288,1152]{1,0:T(8,128)(2,1)S(1)} %get-tuple-element.189.ckv_own), channel_id=1, source_target_pairs={{0,1},{1,0},{2,3},{3,2},{4,5},{5,4},{6,7},{7,6},{8,9},{9,8},{10,11... | collective-permute-start | bytes 1990664 | tf_op jit(solution)/shard_map/ppermute | solution.py:41
  64.1 20.8 %collective-permute-start.12 = (bf16[288,576]{1,0:T(8,128)(2,1)}, bf16[288,576]{1,0:T(8,128)(2,1)S(1)}, u32[]{:S(2)}, u32[]{:S(2)}) collective-permute-start(bf16[288,576]{1,0:T(8,128)(2,1)} %own_m.5), channel_id=1, source_target_pairs={{0,2},{2,0},{4,6},{6,4},{1,3},{3,1},{5,7},{7,5},{8,10},{10,8},{12,... | collective-permute-start | bytes 995336 | tf_op jit(solution)/shard_map/ppermute | solution.py:33
  81.4 16.8 %collective-permute-start.15 = (bf16[120,576]{1,0:T(8,128)(2,1)S(1)}, bf16[120,576]{1,0:T(8,128)(2,1)S(1)}, u32[]{:S(2)}, u32[]{:S(2)}) collective-permute-start(bf16[120,576]{1,0:T(8,128)(2,1)S(1)} %get-tuple-element.461), channel_id=1, source_target_pairs={{0,1},{1,0},{2,3},{3,2},{4,5},{5,4},{6,7},{7,6},{8,9},{9,8},{10,11... | collective-permute-start | bytes 414728 | tf_op jit(solution)/shard_map/ppermute | solution.py:41
  83.4 28.4 %collective-permute-start.19 = (bf16[288,1152]{1,0:T(8,128)(2,1)}, bf16[288,1152]{1,0:T(8,128)(2,1)}, u32[]{:S(2)}, u32[]{:S(2)}) collective-permute-start(bf16[288,1152]{1,0:T(8,128)(2,1)} %collective-permute-done.11.refs_1_), channel_id=1, source_target_pairs={{0,4},{2,6},{4,0},{6,2},{1,5},{3,7},{5,1},{7,3},{8,12},{10,14},{12... | collective-permute-start | bytes 1990664 | tf_op jit(solution)/shard_map/ppermute | solution.py:37
  105.1 49.7 %collective-permute-start.24 = (bf16[576,1152]{1,0:T(8,128)(2,1)}, bf16[576,1152]{1,0:T(8,128)(2,1)}, u32[]{:S(2)}, u32[]{:S(2)}) collective-permute-start(bf16[576,1152]{1,0:T(8,128)(2,1)} %refs_0_.1), channel_id=1, source_target_pairs={{0,1},{1,0},{2,3},{3,2},{4,5},{5,4},{6,7},{7,6},{8,9},{9,8},{10,11... | collective-permute-start | bytes 3981320 | tf_op jit(solution)/shard_map/ppermute | solution.py:41
  107.2 24.5 %collective-permute-start.20 = (bf16[288,1152]{1,0:T(8,128)(2,1)S(1)}, bf16[288,1152]{1,0:T(8,128)(2,1)}, u32[]{:S(2)}, u32[]{:S(2)}) collective-permute-start(bf16[288,1152]{1,0:T(8,128)(2,1)S(1)} %get-tuple-element.184.refs_0_), channel_id=1, source_target_pairs={{0,2},{2,0},{4,6},{6,4},{1,3},{3,1},{5,7},{7,5},{8,10},{10,8},{12,... | collective-permute-start | bytes 1990664 | tf_op jit(solution)/shard_map/ppermute | solution.py:33
  107.4 25.0 %collective-permute-start.21 = (bf16[288,1152]{1,0:T(8,128)(2,1)}, bf16[288,1152]{1,0:T(8,128)(2,1)}, u32[]{:S(2)}, u32[]{:S(2)}) collective-permute-start(bf16[288,1152]{1,0:T(8,128)(2,1)} %collective-permute-done.11.refs_1_), channel_id=1, source_target_pairs={{0,2},{2,0},{4,6},{6,4},{1,3},{3,1},{5,7},{7,5},{8,10},{10,8},{12,... | collective-permute-start | bytes 1990664 | tf_op jit(solution)/shard_map/ppermute | solution.py:33
  108.4 22.0 %collective-permute-start.16 = (bf16[256,1152]{1,0:T(8,128)(2,1)}, bf16[256,1152]{1,0:T(8,128)(2,1)}, u32[]{:S(2)}, u32[]{:S(2)}) collective-permute-start(bf16[256,1152]{1,0:T(8,128)(2,1)} %copy-done.72), channel_id=1, source_target_pairs={{0,4},{2,6},{4,0},{6,2},{1,5},{3,7},{5,1},{7,3},{8,12},{10,14},{12... | collective-permute-start | bytes 1769480 | tf_op jit(solution)/shard_map/ppermute | solution.py:37
  111.8 18.7 %collective-permute-start.18 = (bf16[121,1152]{1,0:T(8,128)(2,1)}, bf16[121,1152]{1,0:T(8,128)(2,1)}, u32[]{:S(2)}, u32[]{:S(2)}) collective-permute-start(bf16[121,1152]{1,0:T(8,128)(2,1)} %pad_maximum_fusion.11), channel_id=1, source_target_pairs={{0,4},{2,6},{4,0},{6,2},{1,5},{3,7},{5,1},{7,3},{8,12},{10,14},{12... | collective-permute-start | bytes 836360 | tf_op jit(solution)/shard_map/ppermute | solution.py:37
  131.7 23.1 %collective-permute-start.25 = (bf16[256,576]{1,0:T(8,128)(2,1)S(1)}, bf16[256,576]{1,0:T(8,128)(2,1)S(1)}, u32[]{:S(2)}, u32[]{:S(2)}) collective-permute-start(bf16[256,576]{1,0:T(8,128)(2,1)S(1)} %get-tuple-element.445), channel_id=1, source_target_pairs={{0,0},{1,4},{2,2},{3,6},{4,1},{5,5},{6,3},{7,7},{8,8},{9,12},{10,1... | collective-permute-start | bytes 884744 | tf_op jit(solution)/shard_map/ppermute | solution.py:75
  132.4 22.4 %collective-permute-start.26 = (bf16[256,576]{1,0:T(8,128)(2,1)S(1)}, bf16[256,576]{1,0:T(8,128)(2,1)S(1)}, u32[]{:S(2)}, u32[]{:S(2)}) collective-permute-start(bf16[256,576]{1,0:T(8,128)(2,1)S(1)} %get-tuple-element.444), channel_id=1, source_target_pairs={{0,4},{1,0},{2,6},{3,2},{4,5},{5,1},{6,7},{7,3},{8,12},{9,8},{10,1... | collective-permute-start | bytes 884744 | tf_op jit(solution)/shard_map/ppermute | solution.py:76
  138.5 33.7 %collective-permute-start.28 = (bf16[576,1152]{1,0:T(8,128)(2,1)S(1)}, bf16[576,1152]{1,0:T(8,128)(2,1)S(1)}, u32[]{:S(2)}, u32[]{:S(2)}) collective-permute-start(bf16[576,1152]{1,0:T(8,128)(2,1)S(1)} %copy-done.3), channel_id=1, source_target_pairs={{0,2},{2,0},{4,6},{6,4},{1,3},{3,1},{5,7},{7,5},{8,10},{10,8},{12,... | collective-permute-start | bytes 3981320 | tf_op jit(solution)/shard_map/ppermute | solution.py:33
  138.6 44.0 %collective-permute-start.31 = (bf16[576,1152]{1,0:T(8,128)(2,1)}, bf16[576,1152]{1,0:T(8,128)(2,1)S(1)}, u32[]{:S(2)}, u32[]{:S(2)}) collective-permute-start(bf16[576,1152]{1,0:T(8,128)(2,1)} %bitcast.42), channel_id=1, source_target_pairs={{0,1},{1,0},{2,3},{3,2},{4,5},{5,4},{6,7},{7,6},{8,9},{9,8},{10,11... | collective-permute-start | bytes 3981320 | tf_op jit(solution)/shard_map/ppermute | solution.py:41
  154.8 15.7 %collective-permute-start.27 = (bf16[256,1152]{1,0:T(8,128)(2,1)S(1)}, bf16[256,1152]{1,0:T(8,128)(2,1)S(1)}, u32[]{:S(2)}, u32[]{:S(2)}) collective-permute-start(bf16[256,1152]{1,0:T(8,128)(2,1)S(1)} %get-tuple-element.203.near), channel_id=1, source_target_pairs={{0,4},{2,6},{4,0},{6,2},{1,5},{3,7},{5,1},{7,3},{8,12},{10,14},{12... | collective-permute-start | bytes 1769480 | tf_op jit(solution)/shard_map/ppermute | solution.py:37
  156.8 15.4 %collective-permute-start.29 = (bf16[576,1152]{1,0:T(8,128)(2,1)}, bf16[576,1152]{1,0:T(8,128)(2,1)S(1)}, u32[]{:S(2)}, u32[]{:S(2)}) collective-permute-start(bf16[576,1152]{1,0:T(8,128)(2,1)} %collective-permute-done.24.got_m.refs_1_), channel_id=1, source_target_pairs={{0,2},{2,0},{4,6},{6,4},{1,3},{3,1},{5,7},{7,5},{8,10},{10,8},{12,... | collective-permute-start | bytes 3981320 | tf_op jit(solution)/shard_map/ppermute | solution.py:33
  170.5 14.9 %collective-permute-start.30 = (bf16[256,1152]{1,0:T(8,128)(2,1)S(1)}, bf16[256,1152]{1,0:T(8,128)(2,1)S(1)}, u32[]{:S(2)}, u32[]{:S(2)}) collective-permute-start(bf16[256,1152]{1,0:T(8,128)(2,1)S(1)} %get-tuple-element.204.g_near.near.gm_ref), channel_id=1, source_target_pairs={{0,4},{2,6},{4,0},{6,2},{1,5},{3,7},{5,1},{7,3},{8,12},{10,14},{12... | collective-permute-start | bytes 1769480 | tf_op jit(solution)/shard_map/ppermute | solution.py:37
  191.9 8.7 %collective-permute-start.32 = (bf16[576,1152]{1,0:T(8,128)(2,1)S(1)}, bf16[576,1152]{1,0:T(8,128)(2,1)S(1)}, u32[]{:S(2)}, u32[]{:S(2)}) collective-permute-start(bf16[576,1152]{1,0:T(8,128)(2,1)S(1)} %bitcast.44), channel_id=1, source_target_pairs={{0,2},{2,0},{4,6},{6,4},{1,3},{3,1},{5,7},{7,5},{8,10},{10,8},{12,... | collective-permute-start | bytes 3981320 | tf_op jit(solution)/shard_map/ppermute | solution.py:33
  192.0 8.6 %collective-permute-start.33 = (bf16[576,1152]{1,0:T(8,128)(2,1)S(1)}, bf16[576,1152]{1,0:T(8,128)(2,1)S(1)}, u32[]{:S(2)}, u32[]{:S(2)}) collective-permute-start(bf16[576,1152]{1,0:T(8,128)(2,1)S(1)} %collective-permute-done.31.refs_5_.got_m), channel_id=1, source_target_pairs={{0,2},{2,0},{4,6},{6,4},{1,3},{3,1},{5,7},{7,5},{8,10},{10,8},{12,... | collective-permute-start | bytes 3981320 | tf_op jit(solution)/shard_map/ppermute | solution.py:33
  199.3 38.1 %collective-permute-start.37 = (bf16[576,1152]{1,0:T(8,128)(2,1)}, bf16[576,1152]{1,0:T(8,128)(2,1)S(1)}, u32[]{:S(2)}, u32[]{:S(2)}) collective-permute-start(bf16[576,1152]{1,0:T(8,128)(2,1)} %add_convert_fusion.8), channel_id=1, source_target_pairs={{0,1},{1,0},{2,3},{3,2},{4,5},{5,4},{6,7},{7,6},{8,9},{9,8},{10,11... | collective-permute-start | bytes 3981320 | tf_op jit(solution)/shard_map/ppermute | solution.py:41
  238.5 16.0 %collective-permute-start.34 = (bf16[256,1152]{1,0:T(8,128)(2,1)}, bf16[256,1152]{1,0:T(8,128)(2,1)S(1)}, u32[]{:S(2)}, u32[]{:S(2)}) collective-permute-start(bf16[256,1152]{1,0:T(8,128)(2,1)} %copy-done.73), channel_id=1, source_target_pairs={{0,4},{2,6},{4,0},{6,2},{1,5},{3,7},{5,1},{7,3},{8,12},{10,14},{12... | collective-permute-start | bytes 1769480 | tf_op jit(solution)/shard_map/ppermute | solution.py:37
  243.8 35.0 %collective-permute-start.41 = (bf16[288,1152]{1,0:T(8,128)(2,1)}, bf16[288,1152]{1,0:T(8,128)(2,1)S(1)}, u32[]{:S(2)}, u32[]{:S(2)}) collective-permute-start(bf16[288,1152]{1,0:T(8,128)(2,1)} %get-tuple-element.419), channel_id=1, source_target_pairs={{0,8},{8,0},{16,24},{24,16},{1,9},{9,1},{17,25},{25,17},{2,10},{10... | collective-permute-start | bytes 1990664 | tf_op jit(solution)/shard_map/ppermute | solution.py:538
  278.7 43.3 %collective-permute-start.40 = (bf16[288,2304]{1,0:T(8,128)(2,1)}, bf16[288,2304]{1,0:T(8,128)(2,1)S(1)}, u32[]{:S(2)}, u32[]{:S(2)}) collective-permute-start(bf16[288,2304]{1,0:T(8,128)(2,1)} %get-tuple-element.238), channel_id=1, source_target_pairs={{0,2},{2,0},{4,6},{6,4},{1,3},{3,1},{5,7},{7,5},{8,10},{10,8},{12,... | collective-permute-start | bytes 3981320 | tf_op jit(solution)/shard_map/ppermute | solution.py:33
  278.9 23.6 %collective-permute-start.42 = (bf16[256,1152]{1,0:T(8,128)(2,1)S(1)}, bf16[256,1152]{1,0:T(8,128)(2,1)S(1)}, u32[]{:S(2)}, u32[]{:S(2)}) collective-permute-start(bf16[256,1152]{1,0:T(8,128)(2,1)S(1)} %get-tuple-element.242.near), channel_id=1, source_target_pairs={{0,4},{2,6},{4,0},{6,2},{1,5},{3,7},{5,1},{7,3},{8,12},{10,14},{12... | collective-permute-start | bytes 1769480 | tf_op jit(solution)/shard_map/ppermute | solution.py:37
  280.4 31.3 %collective-permute-start.43 = (bf16[576,1152]{1,0:T(8,128)(2,1)S(1)}, bf16[576,1152]{1,0:T(8,128)(2,1)S(1)}, u32[]{:S(2)}, u32[]{:S(2)}) collective-permute-start(bf16[576,1152]{1,0:T(8,128)(2,1)S(1)} %add_convert_fusion.6), channel_id=1, source_target_pairs={{0,1},{1,0},{2,3},{3,2},{4,5},{5,4},{6,7},{7,6},{8,9},{9,8},{10,11... | collective-permute-start | bytes 3981320 | tf_op jit(solution)/shard_map/ppermute | solution.py:41
  284.6 17.8 %collective-permute-start.46 = (bf16[144,1152]{1,0:T(8,128)(2,1)S(1)}, bf16[144,1152]{1,0:T(8,128)(2,1)S(1)}, u32[]{:S(2)}, u32[]{:S(2)}) collective-permute-start(bf16[144,1152]{1,0:T(8,128)(2,1)S(1)} %get-tuple-element.436), channel_id=1, source_target_pairs={{0,16},{8,24},{16,0},{24,8},{1,17},{9,25},{17,1},{25,9},{2,18},{10... | collective-permute-start | bytes 995336 | tf_op jit(solution)/shard_map/ppermute | solution.py:538
  311.7 33.9 %collective-permute-start.47 = (bf16[288,2304]{1,0:T(8,128)(2,1)}, bf16[288,2304]{1,0:T(8,128)(2,1)}, u32[]{:S(2)}, u32[]{:S(2)}) collective-permute-start(bf16[288,2304]{1,0:T(8,128)(2,1)} %add_convert_fusion.2), channel_id=1, source_target_pairs={{0,4},{2,6},{4,0},{6,2},{1,5},{3,7},{5,1},{7,3},{8,12},{10,14},{12... | collective-permute-start | bytes 3981320 | tf_op jit(solution)/shard_map/ppermute | solution.py:37
  312.8 32.9 %collective-permute-start.48 = (bf16[120,576]{1,0:T(8,128)(2,1)S(1)}, bf16[120,576]{1,0:T(8,128)(2,1)S(1)}, u32[]{:S(2)}, u32[]{:S(2)}) collective-permute-start(bf16[120,576]{1,0:T(8,128)(2,1)S(1)} %get-tuple-element.465), channel_id=1, source_target_pairs={{0,4},{2,6},{4,0},{6,2},{1,5},{3,7},{5,1},{7,3},{8,12},{10,14},{12... | collective-permute-start | bytes 414728 | tf_op jit(solution)/shard_map/ppermute | solution.py:37
  317.8 27.9 %collective-permute-start.49 = (bf16[288,1152]{1,0:T(8,128)(2,1)S(1)}, bf16[288,1152]{1,0:T(8,128)(2,1)S(1)}, u32[]{:S(2)}, u32[]{:S(2)}) collective-permute-start(bf16[288,1152]{1,0:T(8,128)(2,1)S(1)} %get-tuple-element.258), channel_id=1, source_target_pairs={{0,2},{2,0},{4,6},{6,4},{1,3},{3,1},{5,7},{7,5},{8,10},{10,8},{12,... | collective-permute-start | bytes 1990664 | tf_op jit(solution)/shard_map/ppermute | solution.py:33
  320.5 55.7 %collective-permute-start.51 = (bf16[288,1152]{1,0:T(8,128)(2,1)}, bf16[288,1152]{1,0:T(8,128)(2,1)S(1)}, u32[]{:S(2)}, u32[]{:S(2)}) collective-permute-start(bf16[288,1152]{1,0:T(8,128)(2,1)} %get-tuple-element.417), channel_id=1, source_target_pairs={{0,8},{8,0},{16,24},{24,16},{1,9},{9,1},{17,25},{25,17},{2,10},{10... | collective-permute-start | bytes 1990664 | tf_op jit(solution)/shard_map/ppermute | solution.py:538
  350.6 25.6 %collective-permute-start.50 = (bf16[256,1152]{1,0:T(8,128)(2,1)S(1)}, bf16[256,1152]{1,0:T(8,128)(2,1)S(1)}, u32[]{:S(2)}, u32[]{:S(2)}) collective-permute-start(bf16[256,1152]{1,0:T(8,128)(2,1)S(1)} %copy-done.71), channel_id=1, source_target_pairs={{0,4},{2,6},{4,0},{6,2},{1,5},{3,7},{5,1},{7,3},{8,12},{10,14},{12... | collective-permute-start | bytes 1769480 | tf_op jit(solution)/shard_map/ppermute | solution.py:37
  351.3 24.9 %collective-permute-start.52 = (bf16[144,1152]{1,0:T(8,128)(2,1)S(1)}, bf16[144,1152]{1,0:T(8,128)(2,1)S(1)}, u32[]{:S(2)}, u32[]{:S(2)}) collective-permute-start(bf16[144,1152]{1,0:T(8,128)(2,1)S(1)} %add_convert_fusion.18), channel_id=1, source_target_pairs={{0,16},{8,24},{16,0},{24,8},{1,17},{9,25},{17,1},{25,9},{2,18},{10... | collective-permute-start | bytes 995336 | tf_op jit(solution)/shard_map/ppermute | solution.py:547
  354.4 41.3 %collective-permute-start.54 = (bf16[120,1152]{1,0:T(8,128)(2,1)S(1)}, bf16[120,1152]{1,0:T(8,128)(2,1)S(1)}, u32[]{:S(2)}, u32[]{:S(2)}) collective-permute-start(bf16[120,1152]{1,0:T(8,128)(2,1)S(1)} %get-tuple-element.275), channel_id=1, source_target_pairs={{0,2},{2,0},{4,6},{6,4},{1,3},{3,1},{5,7},{7,5},{8,10},{10,8},{12,... | collective-permute-start | bytes 829448 | tf_op jit(solution)/shard_map/ppermute | solution.py:33
  354.4 52.1 %collective-permute-start.55 = (bf16[288,2880]{1,0:T(8,128)(2,1)}, bf16[288,2880]{1,0:T(8,128)(2,1)S(1)}, u32[]{:S(2)}, u32[]{:S(2)}) collective-permute-start(bf16[288,2880]{1,0:T(8,128)(2,1)} %get-tuple-element.276), channel_id=1, source_target_pairs={{0,1},{1,0},{2,3},{3,2},{4,5},{5,4},{6,7},{7,6},{8,9},{9,8},{10,11... | collective-permute-start | bytes 4976648 | tf_op jit(solution)/shard_map/ppermute | solution.py:41
  376.2 8.9 %collective-permute-start.53 = (bf16[512,1152]{1,0:T(8,128)(2,1)S(1)}, bf16[512,1152]{1,0:T(8,128)(2,1)S(1)}, u32[]{:S(2)}, u32[]{:S(2)}) collective-permute-start(bf16[512,1152]{1,0:T(8,128)(2,1)S(1)} %get-tuple-element.273), channel_id=1, source_target_pairs={{0,2},{2,0},{4,6},{6,4},{1,3},{3,1},{5,7},{7,5},{8,10},{10,8},{12,... | collective-permute-start | bytes 3538952 | tf_op jit(solution)/shard_map/ppermute | solution.py:33
  378.1 19.2 %collective-permute-start.56 = (bf16[256,576]{1,0:T(8,128)(2,1)S(1)}, bf16[256,576]{1,0:T(8,128)(2,1)S(1)}, u32[]{:S(2)}, u32[]{:S(2)}) collective-permute-start(bf16[256,576]{1,0:T(8,128)(2,1)S(1)} %get-tuple-element.453), channel_id=1, source_target_pairs={{0,0},{1,4},{2,2},{3,6},{4,1},{5,5},{6,3},{7,7},{8,8},{9,12},{10,1... | collective-permute-start | bytes 884744 | tf_op jit(solution)/shard_map/ppermute | solution.py:86
  378.8 27.7 %collective-permute-start.57 = (bf16[256,576]{1,0:T(8,128)(2,1)S(1)}, bf16[256,576]{1,0:T(8,128)(2,1)S(1)}, u32[]{:S(2)}, u32[]{:S(2)}) collective-permute-start(bf16[256,576]{1,0:T(8,128)(2,1)S(1)} %get-tuple-element.452), channel_id=1, source_target_pairs={{0,1},{1,5},{2,3},{3,7},{4,0},{5,4},{6,2},{7,6},{8,9},{9,13},{10,1... | collective-permute-start | bytes 884744 | tf_op jit(solution)/shard_map/ppermute | solution.py:87
  385.0 39.7 %collective-permute-start.60 = (bf16[144,1152]{1,0:T(8,128)(2,1)}, bf16[144,1152]{1,0:T(8,128)(2,1)}, u32[]{:S(2)}, u32[]{:S(2)}) collective-permute-start(bf16[144,1152]{1,0:T(8,128)(2,1)} %get-tuple-element.434), channel_id=1, source_target_pairs={{0,16},{8,24},{16,0},{24,8},{1,17},{9,25},{17,1},{25,9},{2,18},{10... | collective-permute-start | bytes 995336 | tf_op jit(solution)/shard_map/ppermute | solution.py:538
  395.7 29.0 %collective-permute-start.61 = (bf16[288,1152]{1,0:T(8,128)(2,1)}, bf16[288,1152]{1,0:T(8,128)(2,1)}, u32[]{:S(2)}, u32[]{:S(2)}) collective-permute-start(bf16[288,1152]{1,0:T(8,128)(2,1)} %pad_maximum_fusion.3), channel_id=1, source_target_pairs={{0,8},{8,0},{16,24},{24,16},{1,9},{9,1},{17,25},{25,17},{2,10},{10... | collective-permute-start | bytes 1990664 | tf_op jit(solution)/shard_map/ppermute | solution.py:547
  408.8 29.4 %collective-permute-start.58 = (bf16[256,1152]{1,0:T(8,128)(2,1)S(1)}, bf16[256,1152]{1,0:T(8,128)(2,1)S(1)}, u32[]{:S(2)}, u32[]{:S(2)}) collective-permute-start(bf16[256,1152]{1,0:T(8,128)(2,1)S(1)} %get-tuple-element.283), channel_id=1, source_target_pairs={{0,4},{2,6},{4,0},{6,2},{1,5},{3,7},{5,1},{7,3},{8,12},{10,14},{12... | collective-permute-start | bytes 1769480 | tf_op jit(solution)/shard_map/ppermute | solution.py:37
  412.1 19.2 %collective-permute-start.59 = (bf16[120,1152]{1,0:T(8,128)(2,1)S(1)}, bf16[120,1152]{1,0:T(8,128)(2,1)S(1)}, u32[]{:S(2)}, u32[]{:S(2)}) collective-permute-start(bf16[120,1152]{1,0:T(8,128)(2,1)S(1)} %fusion), channel_id=1, source_target_pairs={{0,4},{2,6},{4,0},{6,2},{1,5},{3,7},{5,1},{7,3},{8,12},{10,14},{12... | collective-permute-start | bytes 829448 | tf_op jit(solution)/shard_map/ppermute | solution.py:37
  415.7 22.6 %collective-permute-start.63 = (bf16[144,2880]{1,0:T(8,128)(2,1)S(1)}, bf16[144,2880]{1,0:T(8,128)(2,1)S(1)}, u32[]{:S(2)}, u32[]{:S(2)}) collective-permute-start(bf16[144,2880]{1,0:T(8,128)(2,1)S(1)} %get-tuple-element.411), channel_id=1, source_target_pairs={{0,8},{8,0},{16,24},{24,16},{1,9},{9,1},{17,25},{25,17},{2,10},{10... | collective-permute-start | bytes 2488328 | tf_op jit(solution)/shard_map/ppermute | solution.py:538
  432.6 29.0 %collective-permute-start.73 = (bf16[288,1728]{1,0:T(8,128)(2,1)}, bf16[288,1728]{1,0:T(8,128)(2,1)}, u32[]{:S(2)}, u32[]{:S(2)}) collective-permute-start(bf16[288,1728]{1,0:T(8,128)(2,1)} %get-tuple-element.311), channel_id=1, source_target_pairs={{0,2},{2,0},{4,6},{6,4},{1,3},{3,1},{5,7},{7,5},{8,10},{10,8},{12,... | collective-permute-start | bytes 2985992 | tf_op jit(solution)/shard_map/ppermute | solution.py:33
  432.6 69.0 %collective-permute-start.72 = (bf16[288,1728]{1,0:T(8,128)(2,1)}, bf16[288,1728]{1,0:T(8,128)(2,1)}, u32[]{:S(2)}, u32[]{:S(2)}) collective-permute-start(bf16[288,1728]{1,0:T(8,128)(2,1)} %get-tuple-element.309), channel_id=1, source_target_pairs={{0,2},{2,0},{4,6},{6,4},{1,3},{3,1},{5,7},{7,5},{8,10},{10,8},{12,... | collective-permute-start | bytes 2985992 | tf_op jit(solution)/shard_map/ppermute | solution.py:33
  441.5 30.0 %collective-permute-start.64 = (bf16[256,576]{1,0:T(8,128)(2,1)}, bf16[256,576]{1,0:T(8,128)(2,1)}, u32[]{:S(2)}, u32[]{:S(2)}) collective-permute-start(bf16[256,576]{1,0:T(8,128)(2,1)} %get-tuple-element.450), channel_id=1, source_target_pairs={{0,0},{1,4},{2,2},{3,6},{4,1},{5,5},{6,3},{7,7},{8,8},{9,12},{10,1... | collective-permute-start | bytes 884744 | tf_op jit(solution)/shard_map/ppermute | solution.py:86
  466.9 8.9 %collective-permute-start.65 = (bf16[256,576]{1,0:T(8,128)(2,1)S(1)}, bf16[256,576]{1,0:T(8,128)(2,1)S(1)}, u32[]{:S(2)}, u32[]{:S(2)}) collective-permute-start(bf16[256,576]{1,0:T(8,128)(2,1)S(1)} %copy-done.102), channel_id=1, source_target_pairs={{0,1},{1,5},{2,3},{3,7},{4,0},{5,4},{6,2},{7,6},{8,9},{9,13},{10,1... | collective-permute-start | bytes 884744 | tf_op jit(solution)/shard_map/ppermute | solution.py:87
  467.6 33.9 %collective-permute-start.75 = (bf16[72,2880]{1,0:T(8,128)(2,1)}, bf16[72,2880]{1,0:T(8,128)(2,1)}, u32[]{:S(2)}, u32[]{:S(2)}) collective-permute-start(bf16[72,2880]{1,0:T(8,128)(2,1)} %get-tuple-element.428), channel_id=1, source_target_pairs={{0,16},{8,24},{16,0},{24,8},{1,17},{9,25},{17,1},{25,9},{2,18},{10... | collective-permute-start | bytes 1244168 | tf_op jit(solution)/shard_map/ppermute | solution.py:538
  467.8 33.7 %collective-permute-start.74 = (bf16[288,1728]{1,0:T(8,128)(2,1)}, bf16[288,1728]{1,0:T(8,128)(2,1)}, u32[]{:S(2)}, u32[]{:S(2)}) collective-permute-start(bf16[288,1728]{1,0:T(8,128)(2,1)} %add_convert_fusion.10), channel_id=1, source_target_pairs={{0,1},{1,0},{2,3},{3,2},{4,5},{5,4},{6,7},{7,6},{8,9},{9,8},{10,11... | collective-permute-start | bytes 2985992 | tf_op jit(solution)/shard_map/ppermute | solution.py:41
  471.6 30.0 %collective-permute-start.76 = (bf16[144,1152]{1,0:T(8,128)(2,1)S(1)}, bf16[144,1152]{1,0:T(8,128)(2,1)}, u32[]{:S(2)}, u32[]{:S(2)}) collective-permute-start(bf16[144,1152]{1,0:T(8,128)(2,1)S(1)} %copy-done.84), channel_id=1, source_target_pairs={{0,16},{8,24},{16,0},{24,8},{1,17},{9,25},{17,1},{25,9},{2,18},{10... | collective-permute-start | bytes 995336 | tf_op jit(solution)/shard_map/ppermute | solution.py:547
  503.6 24.1 %collective-permute-start.77 = (bf16[144,1728]{1,0:T(8,128)(2,1)S(1)}, bf16[144,1728]{1,0:T(8,128)(2,1)S(1)}, u32[]{:S(2)}, u32[]{:S(2)}) collective-permute-start(bf16[144,1728]{1,0:T(8,128)(2,1)S(1)} %broadcast_select_fusion.14), channel_id=1, source_target_pairs={{0,8},{8,0},{16,24},{24,16},{1,9},{9,1},{17,25},{25,17},{2,10},{10... | collective-permute-start | bytes 1493000 | tf_op jit(solution)/shard_map/ppermute | solution.py:538
  505.6 21.8 %collective-permute-start.81 = (bf16[72,2880]{1,0:T(8,128)(2,1)S(1)}, bf16[72,2880]{1,0:T(8,128)(2,1)S(1)}, u32[]{:S(2)}, u32[]{:S(2)}) collective-permute-start(bf16[72,2880]{1,0:T(8,128)(2,1)S(1)} %add_convert_fusion.16), channel_id=1, source_target_pairs={{0,16},{8,24},{16,0},{24,8},{1,17},{9,25},{17,1},{25,9},{2,18},{10... | collective-permute-start | bytes 1244168 | tf_op jit(solution)/shard_map/ppermute | solution.py:547
  507.8 39.3 %collective-permute-start.83 = (bf16[288,1152]{1,0:T(8,128)(2,1)S(1)}, bf16[288,1152]{1,0:T(8,128)(2,1)S(1)}, u32[]{:S(2)}, u32[]{:S(2)}) collective-permute-start(bf16[288,1152]{1,0:T(8,128)(2,1)S(1)} %pad_maximum_fusion.4), channel_id=1, source_target_pairs={{0,8},{8,0},{16,24},{24,16},{1,9},{9,1},{17,25},{25,17},{2,10},{10... | collective-permute-start | bytes 1990664 | tf_op jit(solution)/shard_map/ppermute | solution.py:547
  527.5 49.5 %collective-permute-start.82 = (bf16[144,2880]{1,0:T(8,128)(2,1)S(1)}, bf16[144,2880]{1,0:T(8,128)(2,1)S(1)}, u32[]{:S(2)}, u32[]{:S(2)}) collective-permute-start(bf16[144,2880]{1,0:T(8,128)(2,1)S(1)} %pad_maximum_fusion), channel_id=1, source_target_pairs={{0,8},{8,0},{16,24},{24,16},{1,9},{9,1},{17,25},{25,17},{2,10},{10... | collective-permute-start | bytes 2488328 | tf_op jit(solution)/shard_map/ppermute | solution.py:547
  527.9 34.2 %collective-permute-start.78 = (bf16[72,1728]{1,0:T(8,128)(2,1)S(1)}, bf16[72,1728]{1,0:T(8,128)(2,1)S(1)}, u32[]{:S(2)}, u32[]{:S(2)}) collective-permute-start(bf16[72,1728]{1,0:T(8,128)(2,1)S(1)} %broadcast_select_fusion.45), channel_id=1, source_target_pairs={{0,16},{8,24},{16,0},{24,8},{1,17},{9,25},{17,1},{25,9},{2,18},{10... | collective-permute-start | bytes 746504 | tf_op jit(solution)/shard_map/ppermute | solution.py:538
  562.2 14.7 %collective-permute-start.79 = (bf16[72,1728]{1,0:T(8,128)(2,1)S(1)}, bf16[72,1728]{1,0:T(8,128)(2,1)S(1)}, u32[]{:S(2)}, u32[]{:S(2)}) collective-permute-start(bf16[72,1728]{1,0:T(8,128)(2,1)S(1)} %add_convert_fusion.20), channel_id=1, source_target_pairs={{0,16},{8,24},{16,0},{24,8},{1,17},{9,25},{17,1},{25,9},{2,18},{10... | collective-permute-start | bytes 746504 | tf_op jit(solution)/shard_map/ppermute | solution.py:547
  577.0 12.5 %collective-permute-start.80 = (bf16[144,1728]{1,0:T(8,128)(2,1)S(1)}, bf16[144,1728]{1,0:T(8,128)(2,1)S(1)}, u32[]{:S(2)}, u32[]{:S(2)}) collective-permute-start(bf16[144,1728]{1,0:T(8,128)(2,1)S(1)} %pad_maximum_fusion.8), channel_id=1, source_target_pairs={{0,8},{8,0},{16,24},{24,16},{1,9},{9,1},{17,25},{25,17},{2,10},{10... | collective-permute-start | bytes 1493000 | tf_op jit(solution)/shard_map/ppermute | solution.py:547
  (148 other events, 1092.8 us)
